TPU v7x, 1024 devices: a whole 8x8x8 slice. The times are simulated.
1024 devices in a mesh: dp: 16 (over y, x_lo), expert: 32 (over z, x_hi), fsdp: 2 (over core).
Axes of the slice: x: 8 (x_hi: 4, x_lo: 2; x = x_hi * 2 + x_lo), y: 8, z: 8, core: 2. Of those that a mesh axis runs over, the one named last changes fastest.
Arguments:
- cotangent: bfloat16 [65536, 2880], P(('dp', 'expert'), 'fsdp'), may hold values from -6 to 6
- route_weight: bfloat16 [65536, 4], P(('dp', 'expert')), may hold values from 0.099609375 to 0.8984375
- expert_ids: int32 [65536, 4], P(('dp', 'expert')), may hold values from 0 to 31, all different within a row; in each aligned block of 128 rows (0 to 127, 128 to 255, ...) at most 20 rows name the same one
- down_weight: bfloat16 [32, 1536, 2880], P('expert', 'fsdp'), may hold values from -0.15625 to 0.15625
- hidden_act: bfloat16 [16, 32, 32, 20, 1536], P('dp', 'expert', None, None, 'fsdp'), may hold values from -0.1875 to 0.1875
Outputs:
- hidden_grad: bfloat16 [16, 32, 32, 20, 1536], P('dp', 'expert', None, None, 'fsdp')
- route_grad: float32 [65536, 4], P(('dp', 'expert'))
Inputs may be any that keep to these rules, and one draw needn't show every extreme that they name: `expert_ids`: among the 128 rows of one block each expert is named at most 20 times, and in every draw some expert is named exactly 20 times by the rows of some block; the 4 experts of a row differ.
All inputs are finite; a program needn't handle non-finite values.
Results may differ from a plain program's by a relative error of at most 0.0065.
Values may be sent and summed in bfloat16 or wider, within the bound.
No kernel may reach another device: no remote copies, remote signals or barrier semaphores. Data moves between devices by JAX's collectives and lax.ppermute only.
A program may use at most 128 MiB of HBM per device.

v0:
```python
import jax
import jax.numpy as jnp
from jax import lax
from jax.sharding import PartitionSpec as P


def slot_table(expert_ids, experts, capacity):
    flat = expert_ids.reshape(-1)
    choices_hit = (flat[:, None] == jnp.arange(experts, dtype=jnp.int32)[None, :]).astype(jnp.int32)
    earlier = jnp.cumsum(choices_hit, axis=0) - choices_hit
    slots = jnp.sum(earlier * choices_hit, axis=1).reshape(expert_ids.shape)
    hit_expert = expert_ids[:, :, None] == jnp.arange(experts, dtype=jnp.int32)[None, None, :]
    hit_slot = slots[:, :, None] == jnp.arange(capacity, dtype=jnp.int32)[None, None, :]
    return (hit_expert[:, :, :, None] & hit_slot[:, :, None, :]).astype(jnp.float32)


def on_device(cotangent, route_weight, expert_ids, down_weight, hidden_act):
    experts = lax.axis_size("expert")
    capacity = hidden_act.shape[3]
    selector = slot_table(expert_ids, experts, capacity)
    placement = jnp.sum(selector, axis=1).astype(jnp.bfloat16)
    send_rows = jnp.einsum(
        "tes,td->esd", placement, cotangent, preferred_element_type=jnp.float32
    ).astype(jnp.bfloat16)
    send_weights = jnp.einsum("tkes,tk->es", selector, route_weight.astype(jnp.float32)).astype(
        jnp.bfloat16
    )
    got_rows, got_weights = (
        lax.all_to_all(send_rows, "expert", split_axis=0, concat_axis=0, tiled=True),
        lax.all_to_all(send_weights, "expert", split_axis=0, concat_axis=0, tiled=True),
    )
    half_width = got_rows.shape[-1]
    flat_rows = got_rows.reshape(-1, half_width)
    col_start = lax.axis_index("fsdp") * half_width
    columns = lax.dynamic_slice_in_dim(
        lax.all_gather(down_weight[0], "fsdp", axis=0, tiled=True), col_start, half_width, 1
    )
    partial_proj = jnp.einsum("rd,hd->rh", flat_rows, columns, preferred_element_type=jnp.float32)
    projected = lax.psum_scatter(partial_proj, "fsdp", scatter_dimension=1, tiled=True)
    projected = projected.reshape(experts, capacity, -1)
    hidden_grad = (got_weights[..., None].astype(jnp.float32) * projected).astype(jnp.bfloat16)
    partial_dots = jnp.sum(hidden_act[0, 0].astype(jnp.float32) * projected, axis=-1)
    whole_dots = lax.psum(partial_dots, "fsdp")
    returned = lax.all_to_all(whole_dots, "expert", split_axis=0, concat_axis=0, tiled=True)
    route_grad = jnp.einsum("tkes,es->tk", selector, returned)
    return (hidden_grad[None, None], route_grad)


def solution(mesh):
    placed = (
        P(("dp", "expert"), "fsdp"),
        P(("dp", "expert"), None),
        P(("dp", "expert"), None),
        P("expert", "fsdp", None),
        P("dp", "expert", None, None, "fsdp"),
    )
    return jax.shard_map(
        on_device,
        mesh=mesh,
        in_specs=placed,
        out_specs=(P("dp", "expert", None, None, "fsdp"), P(("dp", "expert"), None)),
        check_vma=False,
    )
```

profile of v0, /device:TPU:1, one launch (start us, length us, event | category | flops | bytes accessed | tf_op | source)
XLA Modules:
  0.0 176.1 jit_solution(9969153812799235953)
XLA Ops:
  7.2 0.7 all-gather.3.cloned.1.call-update
  8.3 1.2 reduce-window.6
  9.4 0.2 slice_reduce_fusion
  10.2 0.7 convolution_convert_fusion
  10.9 2.6 %copy.39 = bf16[32,20,1440]{2,1,0:T(8,128)(2,1)} copy(bf16[32,20,1440]{2,0,1:T(8,128)(2,1)S(1)} %convolution_convert_fusion) | data formatting | bytes 3686400 | tf_op jit(solution)/shard_map/convert_element_type | solution.py:24
  13.5 22.5 %all-to-all-start.1 = ((bf16[32,20,1440]{2,1,0:T(8,128)(2,1)}), bf16[32,20,1440]{2,1,0:T(8,128)(2,1)S(1)}, u32[]{:S(2)}, u32[]{:S(2)}) async-start(bf16[32,20,1440]{2,1,0:T(8,128)(2,1)} %copy.39), calls=%async_computation.1 | async-start | bytes 4718592 | tf_op jit(solution)/shard_map/all_to_all | solution.py:29
  36.1 63.2 %all-to-all-done.1 = bf16[32,20,1440]{2,1,0:T(8,128)(2,1)S(1)} async-done(((bf16[32,20,1440]{2,1,0:T(8,128)(2,1)}), bf16[32,20,1440]{2,1,0:T(8,128)(2,1)S(1)}, u32[]{:S(2)}, u32[]{:S(2)}) %all-to-all-start.1) | async-done | bytes 1843232 | tf_op jit(solution)/shard_map/all_to_all | solution.py:29
  99.3 2.2 %reshape.65 = bf16[640,1440]{1,0:T(8,128)(2,1)} reshape(bf16[32,20,1440]{2,1,0:T(8,128)(2,1)S(1)} %all-to-all-done.1) | data formatting | bytes 3686400 | tf_op jit(solution)/shard_map/reshape | solution.py:33
  101.5 7.9 %fusion = f32[640,1536]{1,0:T(8,128)} fusion(bf16[640,1440]{1,0:T(8,128)(2,1)} %reshape.65, bf16[1,1536,2880]{1,2,0:T(8,128)(2,1)} %all-gather.3.cloned.1.call-done, s32[]{:T(128)S(6)} %select_n.3), kind=kOutput, calls=%fused_computation | convolution fusion | flops 2831155200 | bytes 10321924 | tf_op jit(solution)/shard_map/rd,hd->rh/dot_general | solution.py:38
  109.5 0.7 copy-done.2
  110.1 0.3 fusion.3
  110.7 0.7 copy.38
  111.4 15.7 %all-to-all-start = ((bf16[32,1,20]{2,1,0:T(2,128)(2,1)}), bf16[32,1,20]{2,1,0:T(2,128)(2,1)S(1)}, u32[]{:S(2)}, u32[]{:S(2)}) async-start(bf16[32,1,20]{2,1,0:T(2,128)(2,1)} %copy.38), calls=%async_computation | async-start | bytes 32768 | tf_op jit(solution)/shard_map/all_to_all | solution.py:30
  127.2 1.8 %copy.40 = f32[1,1,32,20,768]{4,3,2,1,0:T(8,128)S(1)} copy(bf16[1,1,32,20,768]{4,2,3,1,0:T(8,128)(2,1)} %param.9) | data formatting | bytes 2949120 | tf_op jit(solution)/shard_map/convert_element_type | solution.py:42
  128.9 1.4 reshape.69
  130.3 7.7 %all-to-all-done = bf16[32,1,20]{2,1,0:T(2,128)(2,1)S(1)} async-done(((bf16[32,1,20]{2,1,0:T(2,128)(2,1)}), bf16[32,1,20]{2,1,0:T(2,128)(2,1)S(1)}, u32[]{:S(2)}, u32[]{:S(2)}) %all-to-all-start) | async-done | bytes 1312 | tf_op jit(solution)/shard_map/all_to_all | solution.py:30
  138.1 1.7 reduce-scatter.2.cloned.1.call-done
  139.8 2.4 %multiply_reduce_fusion = f32[640]{0:T(1024)S(1)} fusion(f32[640,768]{1,0:T(8,128)} %reshape.69, f32[640,768]{1,0:T(8,128)} %reduce-scatter.2.cloned.1.call-done), kind=kLoop, calls=%fused_computation.9 | loop fusion | flops 982400 | bytes 3934720 | tf_op jit(solution)/shard_map/reduce_sum | solution.py:42
  142.3 4.7 %psum.7 = f32[32,1,20]{2,0,1:T(8,128)} all-reduce(f32[32,1,20]{2,0,1:T(8,128)S(1)} %all_to_all.20), channel_id=1, replica_groups=mesh['dp'=16,'expert'=32,'fsdp'=2] {'fsdp'}, use_global_device_ids=true, to_apply=%region_6.7 | all-reduce | flops 640 | bytes 5120 | tf_op jit(solution)/shard_map/psum | solution.py:43
  146.9 10.4 %all-to-all-start.2 = ((f32[32,1,20]{2,1,0:T(1,128)}), f32[32,1,20]{2,1,0:T(1,128)S(1)}, u32[]{:S(2)}, u32[]{:S(2)}) async-start(f32[32,1,20]{2,1,0:T(1,128)} %bitcast.8), calls=%async_computation.3 | async-start | bytes 32768 | tf_op jit(solution)/shard_map/all_to_all | solution.py:44
  157.4 1.6 reshape.66
  159.2 1.1 copy.42
  160.3 8.0 %all-to-all-done.2 = f32[32,1,20]{2,1,0:T(1,128)S(1)} async-done(((f32[32,1,20]{2,1,0:T(1,128)}), f32[32,1,20]{2,1,0:T(1,128)S(1)}, u32[]{:S(2)}, u32[]{:S(2)}) %all-to-all-start.2) | async-done | bytes 2592 | tf_op jit(solution)/shard_map/all_to_all | solution.py:44
  168.4 0.9 select_reduce_fusion
  (27 shorter events, 1.6 us)
Async XLA Ops:
  7.2 3.1 %copy-start = (bf16[128,1440]{0,1:T(8,128)(2,1)S(1)}, bf16[128,1440]{0,1:T(8,128)(2,1)}, u32[]{:S(2)}) copy-start(bf16[128,1440]{0,1:T(8,128)(2,1)} %param.5) | copy-start | bytes 1105924
  7.2 0.7 copy-start.1
  7.2 94.3 %all-gather.3.cloned.1.call-start = ((), (), s32[]{:S(2)}) async-start(), calls=%async_computation.5 | async-start | bytes 13271040 | tf_op jit(solution)/shard_map/all_gather | solution.py:36
  13.5 85.8 %all-to-all-start.1 = ((bf16[32,20,1440]{2,1,0:T(8,128)(2,1)}), bf16[32,20,1440]{2,1,0:T(8,128)(2,1)S(1)}, u32[]{:S(2)}, u32[]{:S(2)}) async-start(bf16[32,20,1440]{2,1,0:T(8,128)(2,1)} %copy.39), calls=%async_computation.1 | async-start | bytes 4718592 | tf_op jit(solution)/shard_map/all_to_all | solution.py:29
  36.0 103.7 %reduce-scatter.2.cloned.1.call-start = ((), (), s32[]{:S(2)}) async-start(), calls=%async_computation.4 | async-start | bytes 5898240 | tf_op jit(solution)/shard_map/reduce_scatter | solution.py:39
  109.5 0.7 copy-start.2
  111.4 26.7 %all-to-all-start = ((bf16[32,1,20]{2,1,0:T(2,128)(2,1)}), bf16[32,1,20]{2,1,0:T(2,128)(2,1)S(1)}, u32[]{:S(2)}, u32[]{:S(2)}) async-start(bf16[32,1,20]{2,1,0:T(2,128)(2,1)} %copy.38), calls=%async_computation | async-start | bytes 32768 | tf_op jit(solution)/shard_map/all_to_all | solution.py:30
  146.9 21.4 %all-to-all-start.2 = ((f32[32,1,20]{2,1,0:T(1,128)}), f32[32,1,20]{2,1,0:T(1,128)S(1)}, u32[]{:S(2)}, u32[]{:S(2)}) async-start(f32[32,1,20]{2,1,0:T(1,128)} %bitcast.8), calls=%async_computation.3 | async-start | bytes 32768 | tf_op jit(solution)/shard_map/all_to_all | solution.py:44
Sparse Core Ops, SparseCore 0:
  10.7 46.9 all-gather.2
  109.6 30.1 reduce-scatter.1
where the time goes:
time: 177 us; the launch traced here: 176 us
  waiting for transfers between devices  81.3 us (46%)
  starting transfers between devices  48.7 us (28%)
  between operations  14.2 us (8%)
  local copies, waits for them, and re-layouts  13.2 us (7%)
  matrix products  8.94 us (5%)
  other arithmetic  4.99 us (3%)
  blocking collectives  4.68 us (3%)
    all_to_all x1, waiting for transfers between devices, on_device(): lax.all_to_all(send_rows, 'expert', split_axis=0, concat_axis=0, tiled=True)  63.2 us
    all_to_all x1, starting transfers between devices, on_device(): lax.all_to_all(send_rows, 'expert', split_axis=0, concat_axis=0, tiled=True)  22.5 us
    all_to_all x1, starting transfers between devices, on_device(): lax.all_to_all(send_weights, 'expert', split_axis=0, concat_axis=0, tiled...  15.7 us
    all_to_all x1, starting transfers between devices, on_device(): lax.all_to_all(whole_dots, 'expert', split_axis=0, concat_axis=0, tiled=T...  10.4 us
    all_to_all x1, waiting for transfers between devices, on_device(): lax.all_to_all(whole_dots, 'expert', split_axis=0, concat_axis=0, tiled=T...  8.01 us
    dot_general x1, matrix products, on_device(): jnp.einsum('rd,hd->rh', flat_rows, columns, preferred_element_type=jnp.fl...  7.94 us
    all_to_all x1, waiting for transfers between devices, on_device(): lax.all_to_all(send_weights, 'expert', split_axis=0, concat_axis=0, tiled...  7.73 us
    psum x1, blocking collectives, on_device(): whole_dots = lax.psum(partial_dots, 'fsdp')  4.68 us
  transfers between devices with their start and end apart: 5, of which 4 were waited for; matrix products, arithmetic and copies ran while one was open for 9% of the time, Pallas kernels for 0%

commit v1 on v0

v1 whole, which is shorter than its diff:
```python
import jax
import jax.numpy as jnp
from jax import lax
from jax.experimental import pallas as pl
from jax.experimental.pallas import tpu as pltpu
from jax.sharding import PartitionSpec as P

LANES = 128
SUB = 8
FULL = 16
F32 = jnp.float32
BF16 = jnp.bfloat16
NT = (((1,), (1,)), ((), ()))
NN = (((1,), (0,)), ((), ()))


def ranks(ids, experts):
    topk, tokens = ids.shape
    expert = lax.broadcasted_iota(jnp.int32, (experts, tokens), 0)
    hit = jnp.zeros((experts, tokens), F32)
    for k in range(topk):
        hit = hit + (ids[k : k + 1, :] == expert).astype(F32)
    earlier = lax.broadcasted_iota(jnp.int32, (tokens, tokens), 0) < lax.broadcasted_iota(
        jnp.int32, (tokens, tokens), 1
    )
    before = lax.dot_general(
        hit.astype(BF16), earlier.astype(F32).astype(BF16), NN, preferred_element_type=F32
    )
    return jnp.where(hit > 0.5, before, -1.0)


def pack_kernel(ids_ref, weight_ref, cot_ref, send_ref, rank_ref):
    experts = send_ref.shape[0]
    width, tokens = cot_ref.shape
    blocks = -(-width // LANES)
    half = blocks // 2
    whole = width // LANES * LANES
    ids = ids_ref[...]
    rank = ranks(ids, experts)
    rank_ref[...] = rank
    expert = lax.broadcasted_iota(jnp.int32, (experts, tokens), 0)
    gate = jnp.zeros((experts, tokens), F32)
    for k in range(ids.shape[0]):
        gate = gate + jnp.where(
            ids[k : k + 1, :] == expert, weight_ref[k : k + 1, :].astype(F32), 0.0
        )

    cot = cot_ref[...]
    tail = jnp.concatenate(
        [cot[whole:], jnp.zeros((LANES - (width - whole), tokens), BF16)], axis=0
    )
    free = (
        lax.broadcasted_iota(jnp.int32, (LANES, tokens), 0) >= width - whole
    ).astype(F32).astype(BF16)

    def pick(rows, columns):
        return lax.dot_general(rows, columns, NT, preferred_element_type=F32)

    def put(first, count, value):
        send_ref[:, first : first + count, :] = value.astype(BF16).reshape(experts, count, LANES)

    def select(count, wanted):
        rows = lax.broadcasted_iota(jnp.int32, (experts, count, tokens), 1)
        chosen = (rank[:, None, :] == wanted(rows).astype(F32)).astype(F32)
        gated = chosen * gate[:, None, :]
        return (
            chosen.reshape(experts * count, tokens).astype(BF16),
            gated.reshape(experts * count, tokens).astype(BF16),
        )

    rows_a, gated_a = select(FULL, lambda r: r)
    for b in range(blocks - 1):
        put(b * FULL, FULL, pick(rows_a, cot[b * LANES : (b + 1) * LANES]))
    put((blocks - 1) * FULL, FULL, pick(rows_a, tail) + pick(gated_a, free))

    base = blocks * FULL
    rows_l, _ = select(SUB, lambda r: jnp.where(r < SUB // 2, r + FULL, -2))
    rows_h, gated_h = select(SUB, lambda r: jnp.where(r < SUB // 2, -2, r + FULL - SUB // 2))
    for b in range(half):
        low = pick(rows_l, cot[b * LANES : (b + 1) * LANES])
        if half + b < blocks - 1:
            high = pick(rows_h, cot[(half + b) * LANES : (half + b + 1) * LANES])
        else:
            high = pick(rows_h, tail) + pick(gated_h, free)
        put(base + b * SUB, SUB, low + high)


def project_kernel(
    core_ref, own_ref, other_ref, weight_ref, act_ref, grad_ref, dots_ref, part_a, part_b, gate_a, gate_b
):
    sources = own_ref.shape[0]
    depth, hidden = weight_ref.shape
    width = depth // 2
    blocks = -(-width // LANES)
    half = blocks // 2
    whole = width // LANES * LANES
    tail = width - whole
    base = blocks * FULL
    columns = hidden // LANES
    core = core_ref[0]
    mine = core * width
    theirs = width - mine

    def block(ref, first, count):
        return ref[:, first : first + count, :].reshape(sources * count, LANES)

    def weight(first, count):
        return [
            weight_ref[pl.ds(pl.multiple_of(start + first, 16), count), :] for start in (mine, theirs)
        ]

    def mm(rows, columns_):
        return lax.dot_general(
            jnp.concatenate(rows, axis=1),
            jnp.concatenate(columns_, axis=0),
            NN,
            preferred_element_type=F32,
        )

    refs = (own_ref, other_ref)
    tail_w = weight(whole, tail)
    full_a = [[block(ref, b * FULL, FULL) for b in range(blocks - 1)] for ref in refs]
    ends_a = [block(ref, (blocks - 1) * FULL, FULL) for ref in refs]
    out_a = mm(full_a[0] + full_a[1], weight(0, whole)) + mm([x[:, :tail] for x in ends_a], tail_w)
    gate_a[: sources * FULL] = ends_a[0].astype(F32)
    full_b = [[block(ref, base + b * SUB, SUB) for b in range(half)] for ref in refs]
    low_b = mm(full_b[0] + full_b[1], weight(0, half * LANES))
    high_b = mm(
        full_b[0][:-1] + full_b[1][:-1], weight(half * LANES, whole - half * LANES)
    ) + mm([x[-1][:, :tail] for x in full_b], tail_w)
    gate_b[: sources * SUB] = full_b[0][-1].astype(F32)
    for n in range(columns):
        at = slice(n * LANES, (n + 1) * LANES)
        part_a[n, : sources * FULL] = out_a[:, at]
        part_b[0, n, : sources * SUB] = low_b[:, at]
        part_b[1, n, : sources * SUB] = high_b[:, at]

    lane = lax.broadcasted_iota(jnp.int32, (sources, LANES), 1)
    dots = jnp.zeros((sources, LANES), F32)
    for s in range(act_ref.shape[0]):
        total = jnp.zeros((sources, LANES), F32)
        if s < FULL:
            gate = gate_a[pl.ds(s, sources, stride=FULL), :]
        else:
            gate = gate_b[pl.ds(s - FULL + SUB // 2, sources, stride=SUB), :]
        gate = jnp.broadcast_to(gate[:, tail : tail + 1], (sources, LANES))
        for n in range(columns):
            if s < FULL:
                proj = part_a[n, pl.ds(s, sources, stride=FULL), :]
            else:
                proj = (
                    part_b[0, n, pl.ds(s - FULL, sources, stride=SUB), :]
                    + part_b[1, n, pl.ds(s - FULL + SUB // 2, sources, stride=SUB), :]
                )
            at = slice(n * LANES, (n + 1) * LANES)
            grad_ref[s, :, at] = (gate * proj).astype(BF16)
            total = total + act_ref[s, :, at].astype(F32) * proj
        dots = jnp.where(lane == s, jnp.sum(total, axis=1, keepdims=True), dots)
    dots_ref[...] = dots


def collect_kernel(slots, ids_ref, rank_ref, mine_ref, out_ref):
    experts, tokens = rank_ref.shape
    rank = rank_ref[...]
    back = mine_ref[...]
    found = jnp.zeros((experts, tokens), F32)
    for s in range(slots):
        found = jnp.where(rank == float(s), back[:, s : s + 1], found)
    ids = ids_ref[...]
    expert = lax.broadcasted_iota(jnp.int32, (experts, tokens), 0)
    for k in range(ids.shape[0]):
        out_ref[k : k + 1, :] = jnp.sum(
            jnp.where(ids[k : k + 1, :] == expert, found, 0.0), axis=0, keepdims=True
        )


VMEM = pl.BlockSpec(memory_space=pltpu.VMEM)
PARAMS = pltpu.CompilerParams(vmem_limit_bytes=16 * 1024 * 1024)


def on_device(cotangent, route_weight, expert_ids, down_weight, hidden_act):
    experts = lax.axis_size("expert")
    tokens, width = cotangent.shape
    topk = expert_ids.shape[1]
    _, _, _, slots, hidden = hidden_act.shape
    blocks = -(-width // LANES)
    rows = blocks * FULL + blocks // 2 * SUB
    ids = expert_ids.T
    send, rank = pl.pallas_call(
        pack_kernel,
        out_shape=(
            jax.ShapeDtypeStruct((experts, rows, LANES), BF16),
            jax.ShapeDtypeStruct((experts, tokens), F32),
        ),
        in_specs=[VMEM] * 3,
        out_specs=(VMEM, VMEM),
        compiler_params=PARAMS,
        name="pack",
    )(ids, route_weight.T, cotangent.T)
    own = lax.all_to_all(send, "expert", split_axis=0, concat_axis=0, tiled=True)
    other = lax.ppermute(own, "fsdp", [(0, 1), (1, 0)])
    core = lax.axis_index("fsdp").astype(jnp.int32).reshape(1)
    grad, dots = pl.pallas_call(
        project_kernel,
        out_shape=(
            jax.ShapeDtypeStruct((slots, experts, hidden), BF16),
            jax.ShapeDtypeStruct((experts, LANES), F32),
        ),
        in_specs=[pl.BlockSpec(memory_space=pltpu.SMEM)] + [VMEM] * 4,
        out_specs=(VMEM, VMEM),
        scratch_shapes=[
            pltpu.VMEM((hidden // LANES, (experts + 1) * FULL, LANES), F32),
            pltpu.VMEM((2, hidden // LANES, (experts + 1) * SUB, LANES), F32),
            pltpu.VMEM(((experts + 1) * FULL, LANES), F32),
            pltpu.VMEM(((experts + 1) * SUB, LANES), F32),
        ],
        compiler_params=PARAMS,
        name="project",
    )(core, own, other, down_weight[0].T, hidden_act[0, 0].swapaxes(0, 1))
    whole = dots + lax.ppermute(dots, "fsdp", [(0, 1), (1, 0)])
    back = lax.all_to_all(
        whole.reshape(experts, 1, LANES), "expert", split_axis=0, concat_axis=0, tiled=True
    ).reshape(experts, LANES)
    route_grad = pl.pallas_call(
        lambda *refs: collect_kernel(slots, *refs),
        out_shape=jax.ShapeDtypeStruct((topk, tokens), F32),
        in_specs=[VMEM] * 3,
        out_specs=VMEM,
        compiler_params=PARAMS,
        name="collect",
    )(ids, rank, back)
    return grad.swapaxes(0, 1)[None, None], route_grad.T


def solution(mesh):
    placed = (
        P(("dp", "expert"), "fsdp"),
        P(("dp", "expert"), None),
        P(("dp", "expert"), None),
        P("expert", "fsdp", None),
        P("dp", "expert", None, None, "fsdp"),
    )
    return jax.shard_map(
        on_device,
        mesh=mesh,
        in_specs=placed,
        out_specs=(P("dp", "expert", None, None, "fsdp"), P(("dp", "expert"), None)),
        check_vma=False,
    )
```

time: 177 us -> 122 us (0.69)
  blocking collectives: 4.68 us -> 97.5 us
  waiting for transfers between devices: 81.3 us -> 4.52 us
  starting transfers between devices: 48.7 us -> 5.15 us
  between operations: 14.2 us -> 0.68 us
  matrix products: 8.94 us -> 0 us
  Pallas kernels: 0 us -> 8.61 us
  local copies, waits for them, and re-layouts: 13.2 us -> 4.6 us
  other arithmetic: 4.99 us -> 0.01 us
    all_to_all x0 -> x2, blocking collectives: none -> 97.5 us  [the longest x1 79.7 us: on_device(): lax.all_to_all(send, 'expert', split_axis=0, concat_axis=0, tiled=True)]
    all_to_all x3 -> x0, waiting for transfers between devices: 79 us -> none  [the longest x1 63.2 us: on_device(): lax.all_to_all(send_rows, 'expert', split_axis=0, concat_axis=0, tiled=True)]
    all_to_all x3 -> x0, starting transfers between devices: 48.7 us -> none  [the longest x1 22.5 us: on_device(): lax.all_to_all(send_rows, 'expert', split_axis=0, concat_axis=0, tiled=True)]
    dot_general x3 -> x0, matrix products: 8.94 us -> none  [the longest x1 7.94 us: on_device(): jnp.einsum('rd,hd->rh', flat_rows, columns, preferred_element_type=jnp.fl...]
    pallas_call x0 -> x3, Pallas kernels: none -> 8.61 us  [the longest x1 6.87 us: on_device(): pl.pallas_call(project_kernel, out_shape=(jax.ShapeDtypeStruct((slots, ex...]
    convert_element_type x3 -> x0, local copies, waits for them, and re-layouts: 5.77 us -> none  [the longest x2 3.19 us: on_device(): hidden_act[0, 0].astype(jnp.float32) * projected]
    ppermute x0 -> x2, starting transfers between devices: none -> 5.15 us  [the longest x1 2.88 us: on_device(): other = lax.ppermute(own, 'fsdp', [(0, 1), (1, 0)])]
    psum x1 -> x0, blocking collectives: 4.68 us -> none  [on_device(): whole_dots = lax.psum(partial_dots, 'fsdp')]
  transfers between devices with their start and end apart: 5 -> 2, of which waited for: 4 -> 2; matrix products, arithmetic and copies ran while one was open for 9% -> 0% of each run, Pallas kernels for 0% -> 0%
where the time goes in v1:
time: 122 us; the launch traced here: 121 us
  blocking collectives  97.5 us (80%)
  Pallas kernels  8.61 us (7%)
  starting transfers between devices  5.15 us (4%)
  local copies, waits for them, and re-layouts  4.6 us (4%)
  waiting for transfers between devices  4.52 us (4%)
    all_to_all x1, blocking collectives, on_device(): lax.all_to_all(send, 'expert', split_axis=0, concat_axis=0, tiled=True)  79.7 us
    all_to_all x1, blocking collectives, on_device(): lax.all_to_all(whole.reshape(experts, 1, LANES), 'expert', split_axis=0,...  17.8 us
    pallas_call x1, Pallas kernels, on_device(): pl.pallas_call(project_kernel, out_shape=(jax.ShapeDtypeStruct((slots, ex...  6.87 us
    unnamed x12, local copies, waits for them, and re-layouts  4.6 us
    ppermute x1, waiting for transfers between devices, on_device(): other = lax.ppermute(own, 'fsdp', [(0, 1), (1, 0)])  3.7 us
    ppermute x1, starting transfers between devices, on_device(): other = lax.ppermute(own, 'fsdp', [(0, 1), (1, 0)])  2.88 us
  transfers between devices with their start and end apart: 2, of which 2 were waited for; matrix products, arithmetic and copies ran while one was open for 0% of the time, Pallas kernels for 0%

profile of v1, /device:TPU:1, one launch (start us, length us, event | category | flops | bytes accessed | tf_op | source)
XLA Modules:
  0.0 121.1 jit_solution(17827069142178395099)
XLA Ops:
  0.6 0.0 copy-start.2
  0.6 1.0 copy-done.2
  1.6 0.0 copy-start.3
  1.6 0.7 copy-done.3
  2.3 0.0 copy-start.5
  2.3 0.7 copy-done.5
  3.0 1.0 pack.1
  4.0 0.0 copy-start.1
  4.0 79.7 %all_to_all.10.own_ref = bf16[32,240,128]{2,1,0:T(8,128)(2,1)S(1)} all-to-all(bf16[32,240,128]{2,1,0:T(8,128)(2,1)S(1)} %get-tuple-element.6), channel_id=1, replica_groups=mesh['dp'=16,'expert'=32,'fsdp'=2] {'expert'}, dimensions={0} | all-to-all | bytes 3932160 | tf_op jit(solution)/shard_map/all_to_all | solution.py:200
  83.7 2.9 %collective-permute-start = (bf16[32,240,128]{2,1,0:T(8,128)(2,1)S(1)}, bf16[32,240,128]{2,1,0:T(8,128)(2,1)}, u32[]{:S(2)}, u32[]{:S(2)}) collective-permute-start(bf16[32,240,128]{2,1,0:T(8,128)(2,1)S(1)} %all_to_all.10.own_ref), channel_id=1, source_target_pairs={{0,1},{1,0},{2,3},{3,2},{4,5},{5,4},{6,7},{7,6},{8,9},{9,8},{10,11... | collective-permute-start | bytes 5898248 | tf_op jit(solution)/shard_map/ppermute | solution.py:201
  86.6 3.7 %collective-permute-done.other_ref = bf16[32,240,128]{2,1,0:T(8,128)(2,1)} collective-permute-done((bf16[32,240,128]{2,1,0:T(8,128)(2,1)S(1)}, bf16[32,240,128]{2,1,0:T(8,128)(2,1)}, u32[]{:S(2)}, u32[]{:S(2)}) %collective-permute-start) | collective-permute-done | bytes 1966112 | tf_op jit(solution)/shard_map/ppermute | solution.py:201
  90.3 0.0 copy-done.1
  90.3 0.0 copy-start
  90.3 2.3 %copy-done = bf16[1,768,2880]{1,2,0:T(8,128)(2,1)S(1)} copy-done((bf16[1,768,2880]{1,2,0:T(8,128)(2,1)S(1)}, bf16[1,768,2880]{1,2,0:T(8,128)(2,1)}, u32[]{:S(2)}) %copy-start) | copy-done | bytes 4423704
  92.6 0.0 copy-start.4
  92.6 6.9 %project.1 = (bf16[20,32,768]{2,1,0:T(8,128)(2,1)}, f32[32,128]{1,0:T(8,128)S(1)}) custom-call(s32[1]{0:T(128)} %bitcast.core_ref, bf16[32,240,128]{2,1,0:T(8,128)(2,1)S(1)} %all_to_all.10.own_ref, bf16[32,240,128]{2,1,0:T(8,128)(2,1)} %collective-permute-done.other_ref, bf16[2880,768]{1,0:T(8,128)(2,1)S(1)} %bitcast.18, bf16[20,32,768]{2,1,0:T(8,128)(2,1)S(1)} %bitcast.19), custom_call_target="tpu_custom_call" | custom-call | tf_op jit(solution)/shard_map/project/pallas_call | solution.py:203
  99.4 2.3 %collective-permute-start.1 = (f32[32,128]{1,0:T(8,128)S(1)}, f32[32,128]{1,0:T(8,128)S(1)}, u32[]{:S(2)}, u32[]{:S(2)}) collective-permute-start(f32[32,128]{1,0:T(8,128)S(1)} %get-tuple-element.9), channel_id=1, source_target_pairs={{0,1},{1,0},{2,3},{3,2},{4,5},{5,4},{6,7},{7,6},{8,9},{9,8},{10,11... | collective-permute-start | bytes 49160 | tf_op jit(solution)/shard_map/ppermute | solution.py:220
  101.7 0.8 collective-permute-done.1
  102.5 17.8 %all_to_all.11 = f32[32,1,128]{2,1,0:T(1,128)S(1)} all-to-all(f32[32,1,128]{2,1,0:T(1,128)S(1)} %bitcast.25), channel_id=1, replica_groups=mesh['dp'=16,'expert'=32,'fsdp'=2] {'expert'}, dimensions={0} | all-to-all | bytes 32768 | tf_op jit(solution)/shard_map/all_to_all | solution.py:221
  120.3 0.0 copy-done.4
  120.3 0.8 collect.1
  (1 shorter events, 0.0 us)
Async XLA Ops:
  0.6 1.0 copy-start.2
  1.6 0.7 copy-start.3
  2.3 0.7 copy-start.5
  4.0 86.4 %copy-start.1 = (bf16[1,1,32,20,768]{4,2,3,1,0:T(8,128)(2,1)S(1)}, bf16[1,1,32,20,768]{4,2,3,1,0:T(8,128)(2,1)}, u32[]{:S(2)}) copy-start(bf16[1,1,32,20,768]{4,2,3,1,0:T(8,128)(2,1)} %param.9) | copy-start | bytes 2949124
  83.7 6.6 %collective-permute-start = (bf16[32,240,128]{2,1,0:T(8,128)(2,1)S(1)}, bf16[32,240,128]{2,1,0:T(8,128)(2,1)}, u32[]{:S(2)}, u32[]{:S(2)}) collective-permute-start(bf16[32,240,128]{2,1,0:T(8,128)(2,1)S(1)} %all_to_all.10.own_ref), channel_id=1, source_target_pairs={{0,1},{1,0},{2,3},{3,2},{4,5},{5,4},{6,7},{7,6},{8,9},{9,8},{10,11... | collective-permute-start | bytes 5898248 | tf_op jit(solution)/shard_map/ppermute | solution.py:201
  90.3 2.3 %copy-start = (bf16[1,768,2880]{1,2,0:T(8,128)(2,1)S(1)}, bf16[1,768,2880]{1,2,0:T(8,128)(2,1)}, u32[]{:S(2)}) copy-start(bf16[1,768,2880]{1,2,0:T(8,128)(2,1)} %param.8) | copy-start | bytes 13271044
  92.6 27.8 %copy-start.4 = (s32[128,4]{0,1:T(4,128)S(1)}, s32[128,4]{0,1:T(4,128)}, u32[]{:S(2)}) copy-start(s32[128,4]{0,1:T(4,128)} %param.7) | copy-start | bytes 6148
  99.4 3.1 %collective-permute-start.1 = (f32[32,128]{1,0:T(8,128)S(1)}, f32[32,128]{1,0:T(8,128)S(1)}, u32[]{:S(2)}, u32[]{:S(2)}) collective-permute-start(f32[32,128]{1,0:T(8,128)S(1)} %get-tuple-element.9), channel_id=1, source_target_pairs={{0,1},{1,0},{2,3},{3,2},{4,5},{5,4},{6,7},{7,6},{8,9},{9,8},{10,11... | collective-permute-start | bytes 49160 | tf_op jit(solution)/shard_map/ppermute | solution.py:220

commit v2 on v1

--- a/solution.py
+++ b/solution.py
@@ -29,12 +29,25 @@
     return jnp.where(hit > 0.5, before, -1.0)
 
 
-def pack_kernel(ids_ref, weight_ref, cot_ref, send_ref, rank_ref):
+def pack_kernel(
+    ids_hbm, weight_hbm, cot_hbm, sent_hbm, rank_ref, ids_ref, weight_ref, cot_ref, send_ref, in_sems, out_sems
+):
+    inputs = [
+        pltpu.make_async_copy(src, dst, in_sems.at[i])
+        for i, (src, dst) in enumerate(
+            ((ids_hbm, ids_ref), (weight_hbm, weight_ref), (cot_hbm, cot_ref))
+        )
+    ]
+    for copy in inputs:
+        copy.start()
+    outputs = []
     experts = send_ref.shape[0]
     width, tokens = cot_ref.shape
     blocks = -(-width // LANES)
     half = blocks // 2
     whole = width // LANES * LANES
+    inputs[0].wait()
+    inputs[1].wait()
     ids = ids_ref[...]
     rank = ranks(ids, experts)
     rank_ref[...] = rank
@@ -45,6 +58,7 @@
             ids[k : k + 1, :] == expert, weight_ref[k : k + 1, :].astype(F32), 0.0
         )
 
+    inputs[2].wait()
     cot = cot_ref[...]
     tail = jnp.concatenate(
         [cot[whole:], jnp.zeros((LANES - (width - whole), tokens), BF16)], axis=0
@@ -58,6 +72,12 @@
 
     def put(first, count, value):
         send_ref[:, first : first + count, :] = value.astype(BF16).reshape(experts, count, LANES)
+
+    def ship(first, count):
+        at = (slice(None), slice(first, first + count), slice(None))
+        copy = pltpu.make_async_copy(send_ref.at[at], sent_hbm.at[at], out_sems.at[len(outputs)])
+        copy.start()
+        outputs.append(copy)
 
     def select(count, wanted):
         rows = lax.broadcasted_iota(jnp.int32, (experts, count, tokens), 1)
@@ -71,7 +91,9 @@
     rows_a, gated_a = select(FULL, lambda r: r)
     for b in range(blocks - 1):
         put(b * FULL, FULL, pick(rows_a, cot[b * LANES : (b + 1) * LANES]))
+        ship(b * FULL, FULL)
     put((blocks - 1) * FULL, FULL, pick(rows_a, tail) + pick(gated_a, free))
+    ship((blocks - 1) * FULL, FULL)
 
     base = blocks * FULL
     rows_l, _ = select(SUB, lambda r: jnp.where(r < SUB // 2, r + FULL, -2))
@@ -83,10 +105,80 @@
         else:
             high = pick(rows_h, tail) + pick(gated_h, free)
         put(base + b * SUB, SUB, low + high)
+        if b % 2:
+            ship(base + (b - 1) * SUB, 2 * SUB)
+    for copy in outputs:
+        copy.wait()
+
+
+def align_kernel(core_ref, act_ref, act_other_ref, weight_ref, weight_other_ref, out_ref):
+    slots, sources, hidden = act_ref.shape
+    width = weight_ref.shape[0] // 2
+    blocks = -(-width // LANES)
+    half = blocks // 2
+    rows = out_ref.shape[0] // sources
+    start = core_ref[0] * width
+    acts = [ref[...].reshape(slots * sources, hidden) for ref in (act_ref, act_other_ref)]
+    for first in range(0, blocks, 2):
+        at, count = first * LANES, min(2 * LANES, width - first * LANES)
+        out = jnp.zeros((slots * sources, 2 * LANES), F32)
+        for act, ref in zip(acts, (weight_ref, weight_other_ref)):
+            columns = ref[pl.ds(pl.multiple_of(start + at, 16), count), :]
+            if count < 2 * LANES:
+                columns = jnp.concatenate(
+                    [columns, jnp.zeros((2 * LANES - count, hidden), BF16)], axis=0
+                )
+            out = out + lax.dot_general(act, columns, NT, preferred_element_type=F32)
+        for b in (first, first + 1):
+            for s in range(slots):
+                if s < FULL:
+                    row = b * FULL + s
+                else:
+                    row = blocks * FULL + b % half * SUB + b // half * (SUB // 2) + s - FULL
+                out_ref[pl.ds(row, sources, stride=rows), :] = out[
+                    s * sources : (s + 1) * sources, (b - first) * LANES : (b - first + 1) * LANES
+                ]
+
+
+def dots_kernel(blocks, rows_ref, aligned_hbm, dots_ref, aligned_ref, sems):
+    sources = rows_ref.shape[0]
+    parts = sems.shape[0]
+    step = sources // parts
+    copies = [
+        pltpu.make_async_copy(
+            aligned_hbm.at[pl.ds(p * step, step)], aligned_ref.at[pl.ds(p * step, step)], sems.at[p]
+        )
+        for p in range(parts)
+    ]
+    for copy in copies:
+        copy.start()
+
+    def reduce(p, first, count, steps):
+        total = jnp.zeros((step, count, LANES), F32)
+        of = slice(p * step, (p + 1) * step)
+        for b in range(steps):
+            at = slice(first + b * count, first + (b + 1) * count)
+            total = total + rows_ref[of, at, :].astype(F32) * aligned_ref[of, at, :]
+        return jnp.sum(total, axis=2, keepdims=True)
+
+    def spread(value, count, slot):
+        lane = lax.broadcasted_iota(jnp.int32, (step, count, LANES), 2)
+        row = lax.broadcasted_iota(jnp.int32, (step, count, LANES), 1)
+        return jnp.sum(jnp.where(lane == slot(row), value, 0.0), axis=1)
+
+    for p in range(parts):
+        copies[p].wait()
+        full = spread(reduce(p, 0, FULL, blocks), FULL, lambda r: r)
+        split = spread(
+            reduce(p, blocks * FULL, SUB, blocks // 2),
+            SUB,
+            lambda r: jnp.where(r < SUB // 2, r, r - SUB // 2) + FULL,
+        )
+        dots_ref[p * step : (p + 1) * step, :] = full + split
 
 
 def project_kernel(
-    core_ref, own_ref, other_ref, weight_ref, act_ref, grad_ref, dots_ref, part_a, part_b, gate_a, gate_b
+    core_ref, own_ref, other_ref, weight_ref, grad_ref, part_a, part_b, gate_a, gate_b
 ):
     sources = own_ref.shape[0]
     depth, hidden = weight_ref.shape
@@ -135,10 +227,7 @@
         part_b[0, n, : sources * SUB] = low_b[:, at]
         part_b[1, n, : sources * SUB] = high_b[:, at]
 
-    lane = lax.broadcasted_iota(jnp.int32, (sources, LANES), 1)
-    dots = jnp.zeros((sources, LANES), F32)
-    for s in range(act_ref.shape[0]):
-        total = jnp.zeros((sources, LANES), F32)
+    for s in range(grad_ref.shape[0]):
         if s < FULL:
             gate = gate_a[pl.ds(s, sources, stride=FULL), :]
         else:
@@ -154,9 +243,6 @@
                 )
             at = slice(n * LANES, (n + 1) * LANES)
             grad_ref[s, :, at] = (gate * proj).astype(BF16)
-            total = total + act_ref[s, :, at].astype(F32) * proj
-        dots = jnp.where(lane == s, jnp.sum(total, axis=1, keepdims=True), dots)
-    dots_ref[...] = dots
 
 
 def collect_kernel(slots, ids_ref, rank_ref, mine_ref, out_ref):
@@ -175,6 +261,9 @@
 
 
 VMEM = pl.BlockSpec(memory_space=pltpu.VMEM)
+HBM = pl.BlockSpec(memory_space=pltpu.HBM)
+WHOLE = pltpu.CompilerParams(vmem_limit_bytes=64 * 1024 * 1024 - 128 * 1024)
+MOST = pltpu.CompilerParams(vmem_limit_bytes=54 * 1000 * 1000)
 PARAMS = pltpu.CompilerParams(vmem_limit_bytes=16 * 1024 * 1024)
 
 
@@ -192,22 +281,61 @@
             jax.ShapeDtypeStruct((experts, rows, LANES), BF16),
             jax.ShapeDtypeStruct((experts, tokens), F32),
         ),
-        in_specs=[VMEM] * 3,
-        out_specs=(VMEM, VMEM),
-        compiler_params=PARAMS,
+        in_specs=[HBM] * 3,
+        out_specs=(HBM, VMEM),
+        scratch_shapes=[
+            pltpu.VMEM((topk, tokens), jnp.int32),
+            pltpu.VMEM((topk, tokens), BF16),
+            pltpu.VMEM((width, tokens), BF16),
+            pltpu.VMEM((experts, rows, LANES), BF16),
+            pltpu.SemaphoreType.DMA((3,)),
+            pltpu.SemaphoreType.DMA((blocks + blocks // 4,)),
+        ],
+        compiler_params=WHOLE,
         name="pack",
     )(ids, route_weight.T, cotangent.T)
+    weight, send = lax.optimization_barrier((down_weight[0].T, send))
     own = lax.all_to_all(send, "expert", split_axis=0, concat_axis=0, tiled=True)
-    other = lax.ppermute(own, "fsdp", [(0, 1), (1, 0)])
+    swap = [(0, 1), (1, 0)]
     core = lax.axis_index("fsdp").astype(jnp.int32).reshape(1)
-    grad, dots = pl.pallas_call(
+    act = hidden_act[0, 0].swapaxes(0, 1)
+    scalar = pl.BlockSpec(memory_space=pltpu.SMEM)
+    act_other = lax.ppermute(act, "fsdp", swap)
+    weight_other = lax.ppermute(weight, "fsdp", swap)
+    both = pl.pallas_call(
+        align_kernel,
+        out_shape=jax.ShapeDtypeStruct((experts * rows, LANES), F32),
+        in_specs=[scalar] + [VMEM] * 4,
+        out_specs=VMEM,
+        compiler_params=PARAMS,
+        cost_estimate=pl.CostEstimate(
+            flops=2 * slots * experts * weight.size, bytes_accessed=16 * 1024 * 1024, transcendentals=0
+        ),
+        name="align",
+    )(core, act, act_other, weight, weight_other).reshape(experts, rows, LANES)
+    dots = pl.pallas_call(
+        lambda *refs: dots_kernel(blocks, *refs),
+        out_shape=jax.ShapeDtypeStruct((experts, LANES), F32),
+        in_specs=[VMEM, HBM],
+        out_specs=VMEM,
+        scratch_shapes=[
+            pltpu.VMEM((experts, rows, LANES), F32),
+            pltpu.SemaphoreType.DMA((experts // SUB,)),
+        ],
+        compiler_params=MOST,
+        name="dots",
+    )(own, both)
+    own, dots = lax.optimization_barrier((own, dots))
+    whole = dots + lax.ppermute(dots, "fsdp", swap)
+    back = lax.all_to_all(
+        whole.reshape(experts, 1, LANES), "expert", split_axis=0, concat_axis=0, tiled=True
+    ).reshape(experts, LANES)
+    other = lax.ppermute(own, "fsdp", swap)
+    grad = pl.pallas_call(
         project_kernel,
-        out_shape=(
-            jax.ShapeDtypeStruct((slots, experts, hidden), BF16),
-            jax.ShapeDtypeStruct((experts, LANES), F32),
-        ),
-        in_specs=[pl.BlockSpec(memory_space=pltpu.SMEM)] + [VMEM] * 4,
-        out_specs=(VMEM, VMEM),
+        out_shape=jax.ShapeDtypeStruct((slots, experts, hidden), BF16),
+        in_specs=[scalar] + [VMEM] * 3,
+        out_specs=VMEM,
         scratch_shapes=[
             pltpu.VMEM((hidden // LANES, (experts + 1) * FULL, LANES), F32),
             pltpu.VMEM((2, hidden // LANES, (experts + 1) * SUB, LANES), F32),
@@ -215,12 +343,12 @@
             pltpu.VMEM(((experts + 1) * SUB, LANES), F32),
         ],
         compiler_params=PARAMS,
+        cost_estimate=pl.CostEstimate(
+            flops=2 * slots * experts * weight.size, bytes_accessed=10 * 1024 * 1024, transcendentals=0
+        ),
         name="project",
-    )(core, own, other, down_weight[0].T, hidden_act[0, 0].swapaxes(0, 1))
-    whole = dots + lax.ppermute(dots, "fsdp", [(0, 1), (1, 0)])
-    back = lax.all_to_all(
-        whole.reshape(experts, 1, LANES), "expert", split_axis=0, concat_axis=0, tiled=True
-    ).reshape(experts, LANES)
+    )(core, own, other, weight)
+    back, grad = lax.optimization_barrier((back, grad))
     route_grad = pl.pallas_call(
         lambda *refs: collect_kernel(slots, *refs),
         out_shape=jax.ShapeDtypeStruct((topk, tokens), F32),

time: 122 us -> 118 us (0.967)
  blocking collectives: 97.5 us -> 0 us
  waiting for transfers between devices: 4.52 us -> 45.8 us
  starting transfers between devices: 5.15 us -> 43.4 us
  Pallas kernels: 8.61 us -> 20.4 us
  local copies, waits for them, and re-layouts: 4.6 us -> 6.36 us
    all_to_all x2 -> x0, blocking collectives: 97.5 us -> none  [the longest x1 79.7 us: on_device(): lax.all_to_all(send, 'expert', split_axis=0, concat_axis=0, tiled=True)]
    all_to_all x0 -> x2, waiting for transfers between devices: none -> 41.7 us  [the longest x1 39.9 us: on_device(): lax.all_to_all(send, 'expert', split_axis=0, concat_axis=0, tiled=True)]
    all_to_all x0 -> x2, starting transfers between devices: none -> 19.7 us  [the longest x1 10.6 us: on_device(): lax.all_to_all(whole.reshape(experts, 1, LANES), 'expert', split_axis=0,...]
    ppermute x2 -> x4, starting transfers between devices: 5.15 us -> 23.7 us  [the longest x1 16.2 us: on_device(): weight_other = lax.ppermute(weight, 'fsdp', swap)]
    pallas_call x1 -> x3, Pallas kernels: 6.87 us -> 16.3 us  [the longest x1 7.15 us: on_device(): pl.pallas_call(align_kernel, out_shape=jax.ShapeDtypeStruct((experts * ro...]
    pallas_call x1, Pallas kernels: 0.97 us -> 3.33 us  [on_device(): pl.pallas_call(pack_kernel, out_shape=(jax.ShapeDtypeStruct((experts, row...]
    unnamed x12, local copies, waits for them, and re-layouts: 4.6 us -> 6.36 us
    ppermute x2 -> x4, waiting for transfers between devices: 4.52 us -> 4.06 us  [the longest x1 2.38 us: on_device(): act_other = lax.ppermute(act, 'fsdp', swap)]
  transfers between devices with their start and end apart: 2 -> 6, of which waited for: 2 -> 4; matrix products, arithmetic and copies ran while one was open for 0% -> 1% of each run, Pallas kernels for 0% -> 12%
where the time goes in v2:
time: 118 us; the launch traced here: 117 us
  waiting for transfers between devices  45.8 us (39%)
  starting transfers between devices  43.4 us (37%)
  Pallas kernels  20.4 us (17%)
  local copies, waits for them, and re-layouts  6.36 us (5%)
    all_to_all x1, waiting for transfers between devices, on_device(): lax.all_to_all(send, 'expert', split_axis=0, concat_axis=0, tiled=True)  39.9 us
    ppermute x1, starting transfers between devices, on_device(): weight_other = lax.ppermute(weight, 'fsdp', swap)  16.2 us
    all_to_all x1, starting transfers between devices, on_device(): lax.all_to_all(whole.reshape(experts, 1, LANES), 'expert', split_axis=0,...  10.6 us
    all_to_all x1, starting transfers between devices, on_device(): lax.all_to_all(send, 'expert', split_axis=0, concat_axis=0, tiled=True)  9.08 us
    pallas_call x1, Pallas kernels, on_device(): pl.pallas_call(align_kernel, out_shape=jax.ShapeDtypeStruct((experts * ro...  7.15 us
    pallas_call x1, Pallas kernels, on_device(): pl.pallas_call(project_kernel, out_shape=jax.ShapeDtypeStruct((slots, exp...  6.85 us
    unnamed x12, local copies, waits for them, and re-layouts  6.36 us
    ppermute x1, starting transfers between devices, on_device(): other = lax.ppermute(own, 'fsdp', swap)  3.35 us
  transfers between devices with their start and end apart: 6, of which 4 were waited for; matrix products, arithmetic and copies ran while one was open for 1% of the time, Pallas kernels for 12%

profile of v2, /device:TPU:1, one launch (start us, length us, event | category | flops | bytes accessed | tf_op | source)
XLA Modules:
  0.0 117.3 jit_solution(4118198143437121525)
XLA Ops:
  0.6 3.3 %pack.1 = (bf16[32,240,128]{2,1,0:T(8,128)(2,1)}, f32[32,128]{1,0:T(8,128)}) custom-call(s32[4,128]{1,0:T(4,128)} %bitcast.26, bf16[4,128]{1,0:T(4,128)(2,1)} %bitcast.30, bf16[1440,128]{1,0:T(8,128)(2,1)} %bitcast.28), custom_call_target="tpu_custom_call" | custom-call | tf_op jit(solution)/shard_map/pack/pallas_call | solution.py:278
  4.0 0.0 copy-start.3
  4.0 16.2 %collective-permute-start.1 = (bf16[2880,768]{1,0:T(8,128)(2,1)}, bf16[2880,768]{1,0:T(8,128)(2,1)}, u32[]{:S(2)}, u32[]{:S(2)}) collective-permute-start(bf16[2880,768]{1,0:T(8,128)(2,1)} %bitcast.20), channel_id=1, source_target_pairs={{0,1},{1,0},{2,3},{3,2},{4,5},{5,4},{6,7},{7,6},{8,9},{9,8},{10,11... | collective-permute-start | bytes 13271048 | tf_op jit(solution)/shard_map/ppermute | solution.py:304
  20.2 9.1 %all-to-all-start = ((bf16[32,240,128]{2,1,0:T(8,128)(2,1)}), bf16[32,240,128]{2,1,0:T(8,128)(2,1)S(1)}, u32[]{:S(2)}, u32[]{:S(2)}) async-start(bf16[32,240,128]{2,1,0:T(8,128)(2,1)} %get-tuple-element.11), calls=%async_computation | async-start | bytes 3932160 | tf_op jit(solution)/shard_map/all_to_all | solution.py:298
  29.3 2.2 %collective-permute-start = (bf16[20,32,768]{2,1,0:T(8,128)(2,1)S(1)}, bf16[20,32,768]{2,1,0:T(8,128)(2,1)}, u32[]{:S(2)}, u32[]{:S(2)}) collective-permute-start(bf16[20,32,768]{2,1,0:T(8,128)(2,1)S(1)} %bitcast.23), channel_id=1, source_target_pairs={{0,1},{1,0},{2,3},{3,2},{4,5},{5,4},{6,7},{7,6},{8,9},{9,8},{10,11... | collective-permute-start | bytes 2949128 | tf_op jit(solution)/shard_map/ppermute | solution.py:303
  31.5 2.4 %collective-permute-done.act_other_ref = bf16[20,32,768]{2,1,0:T(8,128)(2,1)} collective-permute-done((bf16[20,32,768]{2,1,0:T(8,128)(2,1)S(1)}, bf16[20,32,768]{2,1,0:T(8,128)(2,1)}, u32[]{:S(2)}, u32[]{:S(2)}) %collective-permute-start) | collective-permute-done | bytes 983072 | tf_op jit(solution)/shard_map/ppermute | solution.py:303
  33.9 0.0 collective-permute-done.1.weight_other_ref
  33.9 2.3 %copy-done.1 = bf16[1,768,2880]{1,2,0:T(8,128)(2,1)S(1)} copy-done((bf16[1,768,2880]{1,2,0:T(8,128)(2,1)S(1)}, bf16[1,768,2880]{1,2,0:T(8,128)(2,1)}, u32[]{:S(2)}) %copy-start.1) | copy-done | bytes 4423704
  36.1 7.2 %align.1 = f32[7680,128]{1,0:T(8,128)S(1)} custom-call(s32[1]{0:T(128)} %bitcast.5.core_ref, bf16[20,32,768]{2,1,0:T(8,128)(2,1)S(1)} %bitcast.24, bf16[20,32,768]{2,1,0:T(8,128)(2,1)} %collective-permute-done.act_other_ref, bf16[2880,768]{1,0:T(8,128)(2,1)S(1)} %bitcast.21, bf16[2880,768]{1,0:T(8,128)(2,1)} %collective-permute-done.1.weight_other_ref), custom_call_target="tpu_custom_call" | custom-call | flops 2831155200 | bytes 16777216 | tf_op jit(solution)/shard_map/align/pallas_call | solution.py:305
  43.3 1.8 %copy-done = f32[7680,128]{1,0:T(8,128)} copy-done((f32[7680,128]{1,0:T(8,128)}, f32[7680,128]{1,0:T(8,128)S(1)}, u32[]{:S(2)}) %copy-start) | copy-done | bytes 3932184
  45.1 39.9 %all-to-all-done.refs_0_.own_ref = bf16[32,240,128]{2,1,0:T(8,128)(2,1)S(1)} async-done(((bf16[32,240,128]{2,1,0:T(8,128)(2,1)}), bf16[32,240,128]{2,1,0:T(8,128)(2,1)S(1)}, u32[]{:S(2)}, u32[]{:S(2)}) %all-to-all-start) | async-done | bytes 1966112 | tf_op jit(solution)/shard_map/all_to_all | solution.py:298
  85.0 2.3 %dots.1 = f32[32,128]{1,0:T(8,128)S(1)} custom-call(bf16[32,240,128]{2,1,0:T(8,128)(2,1)S(1)} %all-to-all-done.refs_0_.own_ref, f32[32,240,128]{2,1,0:T(8,128)} %bitcast.19), custom_call_target="tpu_custom_call" | custom-call | tf_op jit(solution)/shard_map/dots/pallas_call | solution.py:316
  87.3 3.3 %collective-permute-start.3 = (bf16[32,240,128]{2,1,0:T(8,128)(2,1)S(1)}, bf16[32,240,128]{2,1,0:T(8,128)(2,1)}, u32[]{:S(2)}, u32[]{:S(2)}) collective-permute-start(bf16[32,240,128]{2,1,0:T(8,128)(2,1)S(1)} %all-to-all-done.refs_0_.own_ref), channel_id=1, source_target_pairs={{0,1},{1,0},{2,3},{3,2},{4,5},{5,4},{6,7},{7,6},{8,9},{9,8},{10,11... | collective-permute-start | bytes 5898248 | tf_op jit(solution)/shard_map/ppermute | solution.py:333
  90.7 1.9 %collective-permute-start.2 = (f32[32,128]{1,0:T(8,128)S(1)}, f32[32,128]{1,0:T(8,128)S(1)}, u32[]{:S(2)}, u32[]{:S(2)}) collective-permute-start(f32[32,128]{1,0:T(8,128)S(1)} %dots.1), channel_id=1, source_target_pairs={{0,1},{1,0},{2,3},{3,2},{4,5},{5,4},{6,7},{7,6},{8,9},{9,8},{10,11... | collective-permute-start | bytes 49160 | tf_op jit(solution)/shard_map/ppermute | solution.py:329
  92.6 1.7 %collective-permute-done.2 = f32[32,128]{1,0:T(8,128)S(1)} collective-permute-done((f32[32,128]{1,0:T(8,128)S(1)}, f32[32,128]{1,0:T(8,128)S(1)}, u32[]{:S(2)}, u32[]{:S(2)}) %collective-permute-start.2) | collective-permute-done | bytes 16416 | tf_op jit(solution)/shard_map/ppermute | solution.py:329
  94.3 0.6 add.3
  94.9 10.6 %all-to-all-start.1 = ((f32[32,1,128]{2,1,0:T(1,128)}), f32[32,1,128]{2,1,0:T(1,128)S(1)}, u32[]{:S(2)}, u32[]{:S(2)}) async-start(f32[32,1,128]{2,1,0:T(1,128)} %bitcast.11), calls=%async_computation.1 | async-start | bytes 32768 | tf_op jit(solution)/shard_map/all_to_all | solution.py:330
  105.5 0.0 collective-permute-done.3.other_ref
  105.5 0.0 copy-start.2
  105.5 2.2 %copy-done.2 = bf16[1,768,2880]{1,2,0:T(8,128)(2,1)S(1)} copy-done((bf16[1,768,2880]{1,2,0:T(8,128)(2,1)S(1)}, bf16[1,768,2880]{1,2,0:T(8,128)(2,1)}, u32[]{:S(2)}) %copy-start.2) | copy-done | bytes 4423704
  107.8 6.9 %project.1 = bf16[20,32,768]{2,1,0:T(8,128)(2,1)} custom-call(s32[1]{0:T(128)} %bitcast.5.core_ref, bf16[32,240,128]{2,1,0:T(8,128)(2,1)S(1)} %all-to-all-done.refs_0_.own_ref, bf16[32,240,128]{2,1,0:T(8,128)(2,1)} %collective-permute-done.3.other_ref, bf16[2880,768]{1,0:T(8,128)(2,1)S(1)} %bitcast.22), custom_call_target="tpu_custom_call" | custom-call | flops 2831155200 | bytes 10485760 | tf_op jit(solution)/shard_map/project/pallas_call | solution.py:334
  114.6 1.9 %all-to-all-done.1 = f32[32,1,128]{2,1,0:T(1,128)S(1)} async-done(((f32[32,1,128]{2,1,0:T(1,128)}), f32[32,1,128]{2,1,0:T(1,128)S(1)}, u32[]{:S(2)}, u32[]{:S(2)}) %all-to-all-start.1) | async-done | bytes 16416 | tf_op jit(solution)/shard_map/all_to_all | solution.py:330
  116.5 0.0 copy-done.4
  116.5 0.8 collect.1
  (6 shorter events, 0.0 us)
Async XLA Ops:
  4.0 25.3 %copy-start.3 = (bf16[1,1,32,20,768]{4,2,3,1,0:T(8,128)(2,1)S(1)}, bf16[1,1,32,20,768]{4,2,3,1,0:T(8,128)(2,1)}, u32[]{:S(2)}) copy-start(bf16[1,1,32,20,768]{4,2,3,1,0:T(8,128)(2,1)} %param.9) | copy-start | bytes 2949124
  4.0 29.9 %collective-permute-start.1 = (bf16[2880,768]{1,0:T(8,128)(2,1)}, bf16[2880,768]{1,0:T(8,128)(2,1)}, u32[]{:S(2)}, u32[]{:S(2)}) collective-permute-start(bf16[2880,768]{1,0:T(8,128)(2,1)} %bitcast.20), channel_id=1, source_target_pairs={{0,1},{1,0},{2,3},{3,2},{4,5},{5,4},{6,7},{7,6},{8,9},{9,8},{10,11... | collective-permute-start | bytes 13271048 | tf_op jit(solution)/shard_map/ppermute | solution.py:304
  20.2 64.8 %all-to-all-start = ((bf16[32,240,128]{2,1,0:T(8,128)(2,1)}), bf16[32,240,128]{2,1,0:T(8,128)(2,1)S(1)}, u32[]{:S(2)}, u32[]{:S(2)}) async-start(bf16[32,240,128]{2,1,0:T(8,128)(2,1)} %get-tuple-element.11), calls=%async_computation | async-start | bytes 3932160 | tf_op jit(solution)/shard_map/all_to_all | solution.py:298
  29.3 4.6 %collective-permute-start = (bf16[20,32,768]{2,1,0:T(8,128)(2,1)S(1)}, bf16[20,32,768]{2,1,0:T(8,128)(2,1)}, u32[]{:S(2)}, u32[]{:S(2)}) collective-permute-start(bf16[20,32,768]{2,1,0:T(8,128)(2,1)S(1)} %bitcast.23), channel_id=1, source_target_pairs={{0,1},{1,0},{2,3},{3,2},{4,5},{5,4},{6,7},{7,6},{8,9},{9,8},{10,11... | collective-permute-start | bytes 2949128 | tf_op jit(solution)/shard_map/ppermute | solution.py:303
  33.9 2.3 %copy-start.1 = (bf16[1,768,2880]{1,2,0:T(8,128)(2,1)S(1)}, bf16[1,768,2880]{1,2,0:T(8,128)(2,1)}, u32[]{:S(2)}) copy-start(bf16[1,768,2880]{1,2,0:T(8,128)(2,1)} %param.8) | copy-start | bytes 13271044
  43.3 1.9 %copy-start = (f32[7680,128]{1,0:T(8,128)}, f32[7680,128]{1,0:T(8,128)S(1)}, u32[]{:S(2)}) copy-start(f32[7680,128]{1,0:T(8,128)S(1)} %align.1) | copy-start | bytes 11796484
  87.3 18.2 %collective-permute-start.3 = (bf16[32,240,128]{2,1,0:T(8,128)(2,1)S(1)}, bf16[32,240,128]{2,1,0:T(8,128)(2,1)}, u32[]{:S(2)}, u32[]{:S(2)}) collective-permute-start(bf16[32,240,128]{2,1,0:T(8,128)(2,1)S(1)} %all-to-all-done.refs_0_.own_ref), channel_id=1, source_target_pairs={{0,1},{1,0},{2,3},{3,2},{4,5},{5,4},{6,7},{7,6},{8,9},{9,8},{10,11... | collective-permute-start | bytes 5898248 | tf_op jit(solution)/shard_map/ppermute | solution.py:333
  90.7 3.6 %collective-permute-start.2 = (f32[32,128]{1,0:T(8,128)S(1)}, f32[32,128]{1,0:T(8,128)S(1)}, u32[]{:S(2)}, u32[]{:S(2)}) collective-permute-start(f32[32,128]{1,0:T(8,128)S(1)} %dots.1), channel_id=1, source_target_pairs={{0,1},{1,0},{2,3},{3,2},{4,5},{5,4},{6,7},{7,6},{8,9},{9,8},{10,11... | collective-permute-start | bytes 49160 | tf_op jit(solution)/shard_map/ppermute | solution.py:329
  94.9 21.6 %all-to-all-start.1 = ((f32[32,1,128]{2,1,0:T(1,128)}), f32[32,1,128]{2,1,0:T(1,128)S(1)}, u32[]{:S(2)}, u32[]{:S(2)}) async-start(f32[32,1,128]{2,1,0:T(1,128)} %bitcast.11), calls=%async_computation.1 | async-start | bytes 32768 | tf_op jit(solution)/shard_map/all_to_all | solution.py:330
  105.5 2.3 %copy-start.2 = (bf16[1,768,2880]{1,2,0:T(8,128)(2,1)S(1)}, bf16[1,768,2880]{1,2,0:T(8,128)(2,1)}, u32[]{:S(2)}) copy-start(bf16[1,768,2880]{1,2,0:T(8,128)(2,1)} %param.8) | copy-start | bytes 13271044
  107.8 8.7 %copy-start.4 = (f32[32,128]{1,0:T(8,128)S(1)}, f32[32,128]{1,0:T(8,128)}, u32[]{:S(2)}) copy-start(f32[32,128]{1,0:T(8,128)} %get-tuple-element.16.refs_1_) | copy-start | bytes 49156
  107.8 8.7 %copy-start.5 = (s32[128,4]{0,1:T(4,128)S(1)}, s32[128,4]{0,1:T(4,128)}, u32[]{:S(2)}) copy-start(s32[128,4]{0,1:T(4,128)} %param.7) | copy-start | bytes 6148

commit v3 on v2

--- a/solution.py
+++ b/solution.py
@@ -174,81 +174,101 @@
             SUB,
             lambda r: jnp.where(r < SUB // 2, r, r - SUB // 2) + FULL,
         )
-        dots_ref[p * step : (p + 1) * step, :] = full + split
+        for first in (p * step, sources + p * step):
+            dots_ref[first : first + step, 0, :] = full + split
 
 
 def project_kernel(
-    core_ref, own_ref, other_ref, weight_ref, grad_ref, part_a, part_b, gate_a, gate_b
+    core_ref, own_ref, other_ref, weight_hbm, grad_hbm, weight_ref, grad_ref, part, tails, gates, in_sems, out_sems
 ):
     sources = own_ref.shape[0]
-    depth, hidden = weight_ref.shape
+    parts, depth, columns = weight_ref.shape
     width = depth // 2
     blocks = -(-width // LANES)
     half = blocks // 2
     whole = width // LANES * LANES
     tail = width - whole
     base = blocks * FULL
-    columns = hidden // LANES
+    split = sources * FULL
     core = core_ref[0]
     mine = core * width
     theirs = width - mine
 
-    def block(ref, first, count):
-        return ref[:, first : first + count, :].reshape(sources * count, LANES)
-
-    def weight(first, count):
-        return [
-            weight_ref[pl.ds(pl.multiple_of(start + first, 16), count), :] for start in (mine, theirs)
-        ]
-
-    def mm(rows, columns_):
-        return lax.dot_general(
-            jnp.concatenate(rows, axis=1),
-            jnp.concatenate(columns_, axis=0),
-            NN,
-            preferred_element_type=F32,
-        )
+    def columns_of(p):
+        return slice(p * columns, (p + 1) * columns)
+
+    inputs = [
+        pltpu.make_async_copy(weight_hbm.at[:, columns_of(p)], weight_ref.at[p], in_sems.at[p])
+        for p in range(parts)
+    ]
+    for copy in inputs:
+        copy.start()
+
+    def block(ref, b):
+        full = ref[:, b * FULL : (b + 1) * FULL, :].reshape(split, LANES)
+        at = base + b % half * SUB
+        return jnp.concatenate([full, ref[:, at : at + SUB, :].reshape(sources * SUB, LANES)], axis=0)
 
     refs = (own_ref, other_ref)
-    tail_w = weight(whole, tail)
-    full_a = [[block(ref, b * FULL, FULL) for b in range(blocks - 1)] for ref in refs]
-    ends_a = [block(ref, (blocks - 1) * FULL, FULL) for ref in refs]
-    out_a = mm(full_a[0] + full_a[1], weight(0, whole)) + mm([x[:, :tail] for x in ends_a], tail_w)
-    gate_a[: sources * FULL] = ends_a[0].astype(F32)
-    full_b = [[block(ref, base + b * SUB, SUB) for b in range(half)] for ref in refs]
-    low_b = mm(full_b[0] + full_b[1], weight(0, half * LANES))
-    high_b = mm(
-        full_b[0][:-1] + full_b[1][:-1], weight(half * LANES, whole - half * LANES)
-    ) + mm([x[-1][:, :tail] for x in full_b], tail_w)
-    gate_b[: sources * SUB] = full_b[0][-1].astype(F32)
-    for n in range(columns):
-        at = slice(n * LANES, (n + 1) * LANES)
-        part_a[n, : sources * FULL] = out_a[:, at]
-        part_b[0, n, : sources * SUB] = low_b[:, at]
-        part_b[1, n, : sources * SUB] = high_b[:, at]
-
-    for s in range(grad_ref.shape[0]):
-        if s < FULL:
-            gate = gate_a[pl.ds(s, sources, stride=FULL), :]
-        else:
-            gate = gate_b[pl.ds(s - FULL + SUB // 2, sources, stride=SUB), :]
-        gate = jnp.broadcast_to(gate[:, tail : tail + 1], (sources, LANES))
-        for n in range(columns):
+    ends = [block(ref, blocks - 1) for ref in refs]
+    low = jnp.concatenate([block(ref, b) for ref in refs for b in range(half)], axis=1)
+    high = jnp.concatenate([block(ref, b) for ref in refs for b in range(half, blocks - 1)], axis=1)
+    last = jnp.concatenate([x[:, :tail] for x in ends], axis=1)
+    gates[: ends[0].shape[0]] = ends[0].astype(F32)
+    outputs = []
+    for p in range(parts):
+        inputs[p].wait()
+
+        def mm(rows, first, count):
+            return lax.dot_general(
+                rows,
+                jnp.concatenate(
+                    [
+                        weight_ref[p, pl.ds(pl.multiple_of(start + first, 16), count), :]
+                        for start in (mine, theirs)
+                    ],
+                    axis=0,
+                ),
+                NN,
+                preferred_element_type=F32,
+            )
+
+        lows = mm(low, 0, half * LANES)
+        highs = mm(high, half * LANES, whole - half * LANES) + mm(last, whole, tail)
+        for n in range(columns // LANES):
+            at = slice(n * LANES, (n + 1) * LANES)
+            part[n, :split] = lows[:split, at] + highs[:split, at]
+            tails[0, n, : sources * SUB] = lows[split:, at]
+            tails[1, n, : sources * SUB] = highs[split:, at]
+        for s in range(grad_ref.shape[0]):
             if s < FULL:
-                proj = part_a[n, pl.ds(s, sources, stride=FULL), :]
+                gate = gates[pl.ds(s, sources, stride=FULL), :]
             else:
-                proj = (
-                    part_b[0, n, pl.ds(s - FULL, sources, stride=SUB), :]
-                    + part_b[1, n, pl.ds(s - FULL + SUB // 2, sources, stride=SUB), :]
-                )
-            at = slice(n * LANES, (n + 1) * LANES)
-            grad_ref[s, :, at] = (gate * proj).astype(BF16)
+                gate = gates[pl.ds(split + s - FULL + SUB // 2, sources, stride=SUB), :]
+            gate = jnp.broadcast_to(gate[:, tail : tail + 1], (sources, LANES))
+            for n in range(columns // LANES):
+                if s < FULL:
+                    proj = part[n, pl.ds(s, sources, stride=FULL), :]
+                else:
+                    proj = (
+                        tails[0, n, pl.ds(s - FULL, sources, stride=SUB), :]
+                        + tails[1, n, pl.ds(s - FULL + SUB // 2, sources, stride=SUB), :]
+                    )
+                at = slice(p * columns + n * LANES, p * columns + (n + 1) * LANES)
+                grad_ref[s, :, at] = (gate * proj).astype(BF16)
+        copy = pltpu.make_async_copy(
+            grad_ref.at[:, :, columns_of(p)], grad_hbm.at[:, :, columns_of(p)], out_sems.at[p]
+        )
+        copy.start()
+        outputs.append(copy)
+    for copy in outputs:
+        copy.wait()
 
 
 def collect_kernel(slots, ids_ref, rank_ref, mine_ref, out_ref):
     experts, tokens = rank_ref.shape
     rank = rank_ref[...]
-    back = mine_ref[...]
+    back = mine_ref[:experts, :] + mine_ref[experts:, :]
     found = jnp.zeros((experts, tokens), F32)
     for s in range(slots):
         found = jnp.where(rank == float(s), back[:, s : s + 1], found)
@@ -264,6 +284,7 @@
 HBM = pl.BlockSpec(memory_space=pltpu.HBM)
 WHOLE = pltpu.CompilerParams(vmem_limit_bytes=64 * 1024 * 1024 - 128 * 1024)
 MOST = pltpu.CompilerParams(vmem_limit_bytes=54 * 1000 * 1000)
+
 PARAMS = pltpu.CompilerParams(vmem_limit_bytes=16 * 1024 * 1024)
 
 
@@ -315,7 +336,7 @@
     )(core, act, act_other, weight, weight_other).reshape(experts, rows, LANES)
     dots = pl.pallas_call(
         lambda *refs: dots_kernel(blocks, *refs),
-        out_shape=jax.ShapeDtypeStruct((experts, LANES), F32),
+        out_shape=jax.ShapeDtypeStruct((2 * experts, 1, LANES), F32),
         in_specs=[VMEM, HBM],
         out_specs=VMEM,
         scratch_shapes=[
@@ -326,23 +347,25 @@
         name="dots",
     )(own, both)
     own, dots = lax.optimization_barrier((own, dots))
-    whole = dots + lax.ppermute(dots, "fsdp", swap)
-    back = lax.all_to_all(
-        whole.reshape(experts, 1, LANES), "expert", split_axis=0, concat_axis=0, tiled=True
-    ).reshape(experts, LANES)
+    back = lax.all_to_all(dots, ("fsdp", "expert"), split_axis=0, concat_axis=0, tiled=True)
+    back = back.reshape(2 * experts, LANES)
     other = lax.ppermute(own, "fsdp", swap)
+    parts = hidden // (2 * LANES)
     grad = pl.pallas_call(
         project_kernel,
         out_shape=jax.ShapeDtypeStruct((slots, experts, hidden), BF16),
-        in_specs=[scalar] + [VMEM] * 3,
-        out_specs=VMEM,
+        in_specs=[scalar, VMEM, VMEM, HBM],
+        out_specs=HBM,
         scratch_shapes=[
-            pltpu.VMEM((hidden // LANES, (experts + 1) * FULL, LANES), F32),
-            pltpu.VMEM((2, hidden // LANES, (experts + 1) * SUB, LANES), F32),
-            pltpu.VMEM(((experts + 1) * FULL, LANES), F32),
-            pltpu.VMEM(((experts + 1) * SUB, LANES), F32),
+            pltpu.VMEM((parts, weight.shape[0], hidden // parts), BF16),
+            pltpu.VMEM((slots, experts, hidden), BF16),
+            pltpu.VMEM((hidden // parts // LANES, (experts + 1) * FULL, LANES), F32),
+            pltpu.VMEM((2, hidden // parts // LANES, (experts + 1) * SUB, LANES), F32),
+            pltpu.VMEM(((experts + 1) * FULL + experts * SUB, LANES), F32),
+            pltpu.SemaphoreType.DMA((parts,)),
+            pltpu.SemaphoreType.DMA((parts,)),
         ],
-        compiler_params=PARAMS,
+        compiler_params=MOST,
         cost_estimate=pl.CostEstimate(
             flops=2 * slots * experts * weight.size, bytes_accessed=10 * 1024 * 1024, transcendentals=0
         ),

time: 118 us -> 115 us (0.975)
  Pallas kernels: 20.4 us -> 24.8 us
  waiting for transfers between devices: 45.8 us -> 43.1 us
  local copies, waits for them, and re-layouts: 6.36 us -> 4.13 us
  starting transfers between devices: 43.4 us -> 42.1 us
    pallas_call x1, Pallas kernels: 6.85 us -> 10.6 us  [on_device(): pl.pallas_call(project_kernel, out_shape=jax.ShapeDtypeStruct((slots, exp...]
    unnamed x12 -> x10, local copies, waits for them, and re-layouts: 6.36 us -> 4.13 us
    ppermute x1 -> x0, starting transfers between devices: 1.92 us -> none  [on_device(): whole = dots + lax.ppermute(dots, 'fsdp', swap)]
    ppermute x1 -> x0, waiting for transfers between devices: 1.67 us -> none  [on_device(): whole = dots + lax.ppermute(dots, 'fsdp', swap)]
  transfers between devices with their start and end apart: 6 -> 5, of which waited for: 4 -> 3; matrix products, arithmetic and copies ran while one was open for 1% -> 0% of each run, Pallas kernels for 12% -> 15%
where the time goes in v3:
time: 115 us
  waiting for transfers between devices  43.1 us (37%)
  starting transfers between devices  42.1 us (37%)
  Pallas kernels  24.8 us (22%)
  local copies, waits for them, and re-layouts  4.13 us (4%)
    all_to_all x1, waiting for transfers between devices, on_device(): lax.all_to_all(send, 'expert', split_axis=0, concat_axis=0, tiled=True)  39.9 us
    ppermute x1, starting transfers between devices, on_device(): weight_other = lax.ppermute(weight, 'fsdp', swap)  16.2 us
    all_to_all x1, starting transfers between devices, on_device(): lax.all_to_all(dots, ('fsdp', 'expert'), split_axis=0, concat_axis=0, til...  11.3 us
    pallas_call x1, Pallas kernels, on_device(): pl.pallas_call(project_kernel, out_shape=jax.ShapeDtypeStruct((slots, exp...  10.6 us
    all_to_all x1, starting transfers between devices, on_device(): lax.all_to_all(send, 'expert', split_axis=0, concat_axis=0, tiled=True)  9.08 us
    pallas_call x1, Pallas kernels, on_device(): pl.pallas_call(align_kernel, out_shape=jax.ShapeDtypeStruct((experts * ro...  7.16 us
    unnamed x10, local copies, waits for them, and re-layouts  4.13 us
    ppermute x1, starting transfers between devices, on_device(): other = lax.ppermute(own, 'fsdp', swap)  3.35 us
  transfers between devices with their start and end apart: 5, of which 3 were waited for; matrix products, arithmetic and copies ran while one was open for 0% of the time, Pallas kernels for 15%

profile of v3, /device:TPU:1, one launch (start us, length us, event | category | flops | bytes accessed | tf_op | source)
XLA Modules:
  0.0 114.9 jit_solution(17469047361454146926)
XLA Ops:
  0.6 3.3 %pack.1 = (bf16[32,240,128]{2,1,0:T(8,128)(2,1)}, f32[32,128]{1,0:T(8,128)}) custom-call(s32[4,128]{1,0:T(4,128)} %bitcast.23, bf16[4,128]{1,0:T(4,128)(2,1)} %bitcast.27, bf16[1440,128]{1,0:T(8,128)(2,1)} %bitcast.25), custom_call_target="tpu_custom_call" | custom-call | tf_op jit(solution)/shard_map/pack/pallas_call | solution.py:299
  4.0 0.0 copy-start.2
  4.0 16.2 %collective-permute-start.1 = (bf16[2880,768]{1,0:T(8,128)(2,1)}, bf16[2880,768]{1,0:T(8,128)(2,1)}, u32[]{:S(2)}, u32[]{:S(2)}) collective-permute-start(bf16[2880,768]{1,0:T(8,128)(2,1)} %bitcast.17), channel_id=1, source_target_pairs={{0,1},{1,0},{2,3},{3,2},{4,5},{5,4},{6,7},{7,6},{8,9},{9,8},{10,11... | collective-permute-start | bytes 13271048 | tf_op jit(solution)/shard_map/ppermute | solution.py:325
  20.2 9.1 %all-to-all-start = ((bf16[32,240,128]{2,1,0:T(8,128)(2,1)}), bf16[32,240,128]{2,1,0:T(8,128)(2,1)S(1)}, u32[]{:S(2)}, u32[]{:S(2)}) async-start(bf16[32,240,128]{2,1,0:T(8,128)(2,1)} %get-tuple-element.11), calls=%async_computation | async-start | bytes 3932160 | tf_op jit(solution)/shard_map/all_to_all | solution.py:319
  29.3 0.0 copy-done.2
  29.3 2.2 %collective-permute-start = (bf16[20,32,768]{2,1,0:T(8,128)(2,1)S(1)}, bf16[20,32,768]{2,1,0:T(8,128)(2,1)}, u32[]{:S(2)}, u32[]{:S(2)}) collective-permute-start(bf16[20,32,768]{2,1,0:T(8,128)(2,1)S(1)} %bitcast.20), channel_id=1, source_target_pairs={{0,1},{1,0},{2,3},{3,2},{4,5},{5,4},{6,7},{7,6},{8,9},{9,8},{10,11... | collective-permute-start | bytes 2949128 | tf_op jit(solution)/shard_map/ppermute | solution.py:324
  31.5 2.4 %collective-permute-done.act_other_ref = bf16[20,32,768]{2,1,0:T(8,128)(2,1)} collective-permute-done((bf16[20,32,768]{2,1,0:T(8,128)(2,1)S(1)}, bf16[20,32,768]{2,1,0:T(8,128)(2,1)}, u32[]{:S(2)}, u32[]{:S(2)}) %collective-permute-start) | collective-permute-done | bytes 983072 | tf_op jit(solution)/shard_map/ppermute | solution.py:324
  33.9 0.0 collective-permute-done.1.weight_other_ref
  33.9 2.3 %copy-done.1 = bf16[1,768,2880]{1,2,0:T(8,128)(2,1)S(1)} copy-done((bf16[1,768,2880]{1,2,0:T(8,128)(2,1)S(1)}, bf16[1,768,2880]{1,2,0:T(8,128)(2,1)}, u32[]{:S(2)}) %copy-start.1) | copy-done | bytes 4423704
  36.1 7.2 %align.1 = f32[7680,128]{1,0:T(8,128)S(1)} custom-call(s32[1]{0:T(128)} %bitcast.5.core_ref, bf16[20,32,768]{2,1,0:T(8,128)(2,1)S(1)} %bitcast.21, bf16[20,32,768]{2,1,0:T(8,128)(2,1)} %collective-permute-done.act_other_ref, bf16[2880,768]{1,0:T(8,128)(2,1)S(1)} %bitcast.19, bf16[2880,768]{1,0:T(8,128)(2,1)} %collective-permute-done.1.weight_other_ref), custom_call_target="tpu_custom_call" | custom-call | flops 2831155200 | bytes 16777216 | tf_op jit(solution)/shard_map/align/pallas_call | solution.py:326
  43.3 0.0 copy-start
  43.3 1.9 %copy-done = f32[7680,128]{1,0:T(8,128)} copy-done((f32[7680,128]{1,0:T(8,128)}, f32[7680,128]{1,0:T(8,128)S(1)}, u32[]{:S(2)}) %copy-start) | copy-done | bytes 3932184
  45.2 39.9 %all-to-all-done.refs_0_.own_ref = bf16[32,240,128]{2,1,0:T(8,128)(2,1)S(1)} async-done(((bf16[32,240,128]{2,1,0:T(8,128)(2,1)}), bf16[32,240,128]{2,1,0:T(8,128)(2,1)S(1)}, u32[]{:S(2)}, u32[]{:S(2)}) %all-to-all-start) | async-done | bytes 1966112 | tf_op jit(solution)/shard_map/all_to_all | solution.py:319
  85.0 2.9 %dots.1 = f32[64,1,128]{2,1,0:T(1,128)} custom-call(bf16[32,240,128]{2,1,0:T(8,128)(2,1)S(1)} %all-to-all-done.refs_0_.own_ref, f32[32,240,128]{2,1,0:T(8,128)} %bitcast.16), custom_call_target="tpu_custom_call" | custom-call | tf_op jit(solution)/shard_map/dots/pallas_call | solution.py:337
  87.9 3.3 %collective-permute-start.2 = (bf16[32,240,128]{2,1,0:T(8,128)(2,1)S(1)}, bf16[32,240,128]{2,1,0:T(8,128)(2,1)}, u32[]{:S(2)}, u32[]{:S(2)}) collective-permute-start(bf16[32,240,128]{2,1,0:T(8,128)(2,1)S(1)} %all-to-all-done.refs_0_.own_ref), channel_id=1, source_target_pairs={{0,1},{1,0},{2,3},{3,2},{4,5},{5,4},{6,7},{7,6},{8,9},{9,8},{10,11... | collective-permute-start | bytes 5898248 | tf_op jit(solution)/shard_map/ppermute | solution.py:352
  91.3 11.3 %all-to-all-start.1 = ((f32[64,1,128]{2,1,0:T(1,128)}), f32[64,1,128]{2,1,0:T(1,128)S(1)}, u32[]{:S(2)}, u32[]{:S(2)}) async-start(f32[64,1,128]{2,1,0:T(1,128)} %dots.1), calls=%async_computation.1 | async-start | bytes 65536 | tf_op jit(solution)/shard_map/all_to_all | solution.py:350
  102.6 0.0 copy-start.3
  102.6 0.0 copy-start.4
  102.6 0.0 collective-permute-done.2.other_ref
  102.6 10.6 %project.1 = bf16[20,32,768]{2,1,0:T(8,128)(2,1)} custom-call(s32[1]{0:T(128)} %bitcast.5.core_ref, bf16[32,240,128]{2,1,0:T(8,128)(2,1)S(1)} %all-to-all-done.refs_0_.own_ref, bf16[32,240,128]{2,1,0:T(8,128)(2,1)} %collective-permute-done.2.other_ref, bf16[2880,768]{1,0:T(8,128)(2,1)} %bitcast.18), custom_call_target="tpu_custom_call" | custom-call | flops 2831155200 | bytes 10485760 | tf_op jit(solution)/shard_map/project/pallas_call | solution.py:354
  113.2 0.8 all-to-all-done.1
  114.1 0.0 copy-done.3
  114.1 0.0 copy-done.4
  114.1 0.8 collect.1
  (1 shorter events, 0.0 us)
Async XLA Ops:
  4.0 25.3 %copy-start.2 = (bf16[1,1,32,20,768]{4,2,3,1,0:T(8,128)(2,1)S(1)}, bf16[1,1,32,20,768]{4,2,3,1,0:T(8,128)(2,1)}, u32[]{:S(2)}) copy-start(bf16[1,1,32,20,768]{4,2,3,1,0:T(8,128)(2,1)} %param.9) | copy-start | bytes 2949124
  4.0 29.9 %collective-permute-start.1 = (bf16[2880,768]{1,0:T(8,128)(2,1)}, bf16[2880,768]{1,0:T(8,128)(2,1)}, u32[]{:S(2)}, u32[]{:S(2)}) collective-permute-start(bf16[2880,768]{1,0:T(8,128)(2,1)} %bitcast.17), channel_id=1, source_target_pairs={{0,1},{1,0},{2,3},{3,2},{4,5},{5,4},{6,7},{7,6},{8,9},{9,8},{10,11... | collective-permute-start | bytes 13271048 | tf_op jit(solution)/shard_map/ppermute | solution.py:325
  20.2 64.8 %all-to-all-start = ((bf16[32,240,128]{2,1,0:T(8,128)(2,1)}), bf16[32,240,128]{2,1,0:T(8,128)(2,1)S(1)}, u32[]{:S(2)}, u32[]{:S(2)}) async-start(bf16[32,240,128]{2,1,0:T(8,128)(2,1)} %get-tuple-element.11), calls=%async_computation | async-start | bytes 3932160 | tf_op jit(solution)/shard_map/all_to_all | solution.py:319
  29.3 4.6 %collective-permute-start = (bf16[20,32,768]{2,1,0:T(8,128)(2,1)S(1)}, bf16[20,32,768]{2,1,0:T(8,128)(2,1)}, u32[]{:S(2)}, u32[]{:S(2)}) collective-permute-start(bf16[20,32,768]{2,1,0:T(8,128)(2,1)S(1)} %bitcast.20), channel_id=1, source_target_pairs={{0,1},{1,0},{2,3},{3,2},{4,5},{5,4},{6,7},{7,6},{8,9},{9,8},{10,11... | collective-permute-start | bytes 2949128 | tf_op jit(solution)/shard_map/ppermute | solution.py:324
  33.9 2.3 %copy-start.1 = (bf16[1,768,2880]{1,2,0:T(8,128)(2,1)S(1)}, bf16[1,768,2880]{1,2,0:T(8,128)(2,1)}, u32[]{:S(2)}) copy-start(bf16[1,768,2880]{1,2,0:T(8,128)(2,1)} %param.8) | copy-start | bytes 13271044
  43.3 1.9 %copy-start = (f32[7680,128]{1,0:T(8,128)}, f32[7680,128]{1,0:T(8,128)S(1)}, u32[]{:S(2)}) copy-start(f32[7680,128]{1,0:T(8,128)S(1)} %align.1) | copy-start | bytes 11796484
  87.9 14.7 %collective-permute-start.2 = (bf16[32,240,128]{2,1,0:T(8,128)(2,1)S(1)}, bf16[32,240,128]{2,1,0:T(8,128)(2,1)}, u32[]{:S(2)}, u32[]{:S(2)}) collective-permute-start(bf16[32,240,128]{2,1,0:T(8,128)(2,1)S(1)} %all-to-all-done.refs_0_.own_ref), channel_id=1, source_target_pairs={{0,1},{1,0},{2,3},{3,2},{4,5},{5,4},{6,7},{7,6},{8,9},{9,8},{10,11... | collective-permute-start | bytes 5898248 | tf_op jit(solution)/shard_map/ppermute | solution.py:352
  91.3 22.8 %all-to-all-start.1 = ((f32[64,1,128]{2,1,0:T(1,128)}), f32[64,1,128]{2,1,0:T(1,128)S(1)}, u32[]{:S(2)}, u32[]{:S(2)}) async-start(f32[64,1,128]{2,1,0:T(1,128)} %dots.1), calls=%async_computation.1 | async-start | bytes 65536 | tf_op jit(solution)/shard_map/all_to_all | solution.py:350
  102.6 11.5 %copy-start.3 = (f32[32,128]{1,0:T(8,128)S(1)}, f32[32,128]{1,0:T(8,128)}, u32[]{:S(2)}) copy-start(f32[32,128]{1,0:T(8,128)} %get-tuple-element.16.refs_1_) | copy-start | bytes 49156
  102.6 11.5 %copy-start.4 = (s32[128,4]{0,1:T(4,128)S(1)}, s32[128,4]{0,1:T(4,128)}, u32[]{:S(2)}) copy-start(s32[128,4]{0,1:T(4,128)} %param.7) | copy-start | bytes 6148

commit v4 on v2

--- a/solution.py
+++ b/solution.py
@@ -111,7 +111,7 @@
         copy.wait()
 
 
-def align_kernel(core_ref, act_ref, act_other_ref, weight_ref, weight_other_ref, out_ref):
+def align_kernel(core_ref, act_ref, act_other_ref, weight_ref, other_low_ref, other_high_ref, out_ref):
     slots, sources, hidden = act_ref.shape
     width = weight_ref.shape[0] // 2
     blocks = -(-width // LANES)
@@ -122,8 +122,15 @@
     for first in range(0, blocks, 2):
         at, count = first * LANES, min(2 * LANES, width - first * LANES)
         out = jnp.zeros((slots * sources, 2 * LANES), F32)
-        for act, ref in zip(acts, (weight_ref, weight_other_ref)):
-            columns = ref[pl.ds(pl.multiple_of(start + at, 16), count), :]
+        for c, act in enumerate(acts):
+            if c:
+                cut = other_low_ref.shape[0]
+                columns = [other_low_ref[at : at + count, :]] if at < cut else []
+                if at + count > cut:
+                    columns.append(other_high_ref[max(at - cut, 0) : at + count - cut, :])
+                columns = jnp.concatenate(columns, axis=0)
+            else:
+                columns = weight_ref[pl.ds(pl.multiple_of(start + at, 16), count), :]
             if count < 2 * LANES:
                 columns = jnp.concatenate(
                     [columns, jnp.zeros((2 * LANES - count, hidden), BF16)], axis=0
@@ -174,81 +181,106 @@
             SUB,
             lambda r: jnp.where(r < SUB // 2, r, r - SUB // 2) + FULL,
         )
-        dots_ref[p * step : (p + 1) * step, :] = full + split
+        for first in (p * step, sources + p * step):
+            dots_ref[first : first + step, :] = full + split
 
 
 def project_kernel(
-    core_ref, own_ref, other_ref, weight_ref, grad_ref, part_a, part_b, gate_a, gate_b
+    core_ref, own_ref, other_hbm, weight_hbm, grad_hbm, weight_ref, other_ref, grad_ref, part, tails, gates, in_sems, out_sems
 ):
     sources = own_ref.shape[0]
-    depth, hidden = weight_ref.shape
-    width = depth // 2
+    _, width, hidden = weight_ref.shape
+    slots = grad_ref.shape[0]
+    columns = hidden // LANES
     blocks = -(-width // LANES)
     half = blocks // 2
-    whole = width // LANES * LANES
-    tail = width - whole
+    tail = width % LANES
     base = blocks * FULL
-    columns = hidden // LANES
-    core = core_ref[0]
-    mine = core * width
-    theirs = width - mine
+    split = sources * FULL
+    mine = core_ref[0] * width
+
+    def fetch(i, src, dst):
+        copy = pltpu.make_async_copy(src, dst, in_sems.at[i])
+        copy.start()
+        return copy
+
+    def weight_rows(start, count):
+        return weight_hbm.at[pl.ds(pl.multiple_of(start, 16), count)]
+
+    cut = half * LANES
+    inputs = (
+        fetch(0, weight_rows(mine, cut), weight_ref.at[0, :cut]),
+        fetch(1, weight_rows(mine + cut, width - cut), weight_ref.at[0, cut:]),
+        fetch(2, other_hbm, other_ref),
+        fetch(3, weight_rows(width - mine, cut), weight_ref.at[1, :cut]),
+        fetch(4, weight_rows(width - mine + cut, width - cut), weight_ref.at[1, cut:]),
+    )
 
     def block(ref, first, count):
         return ref[:, first : first + count, :].reshape(sources * count, LANES)
 
-    def weight(first, count):
-        return [
-            weight_ref[pl.ds(pl.multiple_of(start + first, 16), count), :] for start in (mine, theirs)
-        ]
-
-    def mm(rows, columns_):
-        return lax.dot_general(
-            jnp.concatenate(rows, axis=1),
-            jnp.concatenate(columns_, axis=0),
-            NN,
-            preferred_element_type=F32,
-        )
-
-    refs = (own_ref, other_ref)
-    tail_w = weight(whole, tail)
-    full_a = [[block(ref, b * FULL, FULL) for b in range(blocks - 1)] for ref in refs]
-    ends_a = [block(ref, (blocks - 1) * FULL, FULL) for ref in refs]
-    out_a = mm(full_a[0] + full_a[1], weight(0, whole)) + mm([x[:, :tail] for x in ends_a], tail_w)
-    gate_a[: sources * FULL] = ends_a[0].astype(F32)
-    full_b = [[block(ref, base + b * SUB, SUB) for b in range(half)] for ref in refs]
-    low_b = mm(full_b[0] + full_b[1], weight(0, half * LANES))
-    high_b = mm(
-        full_b[0][:-1] + full_b[1][:-1], weight(half * LANES, whole - half * LANES)
-    ) + mm([x[-1][:, :tail] for x in full_b], tail_w)
-    gate_b[: sources * SUB] = full_b[0][-1].astype(F32)
-    for n in range(columns):
-        at = slice(n * LANES, (n + 1) * LANES)
-        part_a[n, : sources * FULL] = out_a[:, at]
-        part_b[0, n, : sources * SUB] = low_b[:, at]
-        part_b[1, n, : sources * SUB] = high_b[:, at]
-
-    for s in range(grad_ref.shape[0]):
+    def lanes(n):
+        return slice(n * LANES, (n + 1) * LANES)
+
+    def product(ref, c, h):
+        last = width - cut if h else cut
+
+        def dot(first, count):
+            rows = [block(ref, first + b * count, count) for b in range(half)]
+            return lax.dot_general(
+                jnp.concatenate(rows, axis=1)[:, :last],
+                weight_ref[c, h * cut : h * cut + last, :],
+                NN,
+                preferred_element_type=F32,
+            )
+
+        return dot(h * half * FULL, FULL), dot(base, SUB)
+
+    gates[:split] = block(own_ref, (blocks - 1) * FULL, FULL).astype(F32)
+    gates[split : split + sources * SUB] = block(own_ref, base + (half - 1) * SUB, SUB).astype(F32)
+    for c, ref in enumerate((own_ref, other_ref)):
+        for h in (0, 1):
+            if c == 1 and h == 0:
+                inputs[2].wait()
+            inputs[3 * c + h].wait()
+            out, some = product(ref, c, h)
+            for n in range(columns):
+                full = out[:, lanes(n)]
+                few = some[:, lanes(n)]
+                if c or h:
+                    full = full + part[n, :split]
+                if c:
+                    few = few + tails[h, n, : sources * SUB]
+                part[n, :split] = full
+                tails[h, n, : sources * SUB] = few
+
+    outputs = []
+    for s in range(slots):
         if s < FULL:
-            gate = gate_a[pl.ds(s, sources, stride=FULL), :]
+            gate = gates[pl.ds(s, sources, stride=FULL), :]
         else:
-            gate = gate_b[pl.ds(s - FULL + SUB // 2, sources, stride=SUB), :]
+            gate = gates[pl.ds(split + s - FULL + SUB // 2, sources, stride=SUB), :]
         gate = jnp.broadcast_to(gate[:, tail : tail + 1], (sources, LANES))
         for n in range(columns):
             if s < FULL:
-                proj = part_a[n, pl.ds(s, sources, stride=FULL), :]
+                proj = part[n, pl.ds(s, sources, stride=FULL), :]
             else:
                 proj = (
-                    part_b[0, n, pl.ds(s - FULL, sources, stride=SUB), :]
-                    + part_b[1, n, pl.ds(s - FULL + SUB // 2, sources, stride=SUB), :]
+                    tails[0, n, pl.ds(s - FULL, sources, stride=SUB), :]
+                    + tails[1, n, pl.ds(s - FULL + SUB // 2, sources, stride=SUB), :]
                 )
-            at = slice(n * LANES, (n + 1) * LANES)
-            grad_ref[s, :, at] = (gate * proj).astype(BF16)
+            grad_ref[s, :, lanes(n)] = (gate * proj).astype(BF16)
+        copy = pltpu.make_async_copy(grad_ref.at[s], grad_hbm.at[s], out_sems.at[s])
+        copy.start()
+        outputs.append(copy)
+    for copy in outputs:
+        copy.wait()
 
 
 def collect_kernel(slots, ids_ref, rank_ref, mine_ref, out_ref):
     experts, tokens = rank_ref.shape
     rank = rank_ref[...]
-    back = mine_ref[...]
+    back = mine_ref[:experts, :] + mine_ref[experts:, :]
     found = jnp.zeros((experts, tokens), F32)
     for s in range(slots):
         found = jnp.where(rank == float(s), back[:, s : s + 1], found)
@@ -264,6 +296,7 @@
 HBM = pl.BlockSpec(memory_space=pltpu.HBM)
 WHOLE = pltpu.CompilerParams(vmem_limit_bytes=64 * 1024 * 1024 - 128 * 1024)
 MOST = pltpu.CompilerParams(vmem_limit_bytes=54 * 1000 * 1000)
+
 PARAMS = pltpu.CompilerParams(vmem_limit_bytes=16 * 1024 * 1024)
 
 
@@ -301,21 +334,26 @@
     act = hidden_act[0, 0].swapaxes(0, 1)
     scalar = pl.BlockSpec(memory_space=pltpu.SMEM)
     act_other = lax.ppermute(act, "fsdp", swap)
-    weight_other = lax.ppermute(weight, "fsdp", swap)
+    start = (1 - core[0]) * width
+    cut = width // 2
+    weight_other = [
+        lax.ppermute(lax.dynamic_slice_in_dim(weight, start + first, cut, 0), "fsdp", swap)
+        for first in (0, cut)
+    ]
     both = pl.pallas_call(
         align_kernel,
         out_shape=jax.ShapeDtypeStruct((experts * rows, LANES), F32),
-        in_specs=[scalar] + [VMEM] * 4,
+        in_specs=[scalar] + [VMEM] * 5,
         out_specs=VMEM,
         compiler_params=PARAMS,
         cost_estimate=pl.CostEstimate(
             flops=2 * slots * experts * weight.size, bytes_accessed=16 * 1024 * 1024, transcendentals=0
         ),
         name="align",
-    )(core, act, act_other, weight, weight_other).reshape(experts, rows, LANES)
+    )(core, act, act_other, weight, *weight_other).reshape(experts, rows, LANES)
     dots = pl.pallas_call(
         lambda *refs: dots_kernel(blocks, *refs),
-        out_shape=jax.ShapeDtypeStruct((experts, LANES), F32),
+        out_shape=jax.ShapeDtypeStruct((2 * experts, LANES), F32),
         in_specs=[VMEM, HBM],
         out_specs=VMEM,
         scratch_shapes=[
@@ -324,25 +362,27 @@
         ],
         compiler_params=MOST,
         name="dots",
-    )(own, both)
+    )(own, both).reshape(2 * experts, 1, LANES)
     own, dots = lax.optimization_barrier((own, dots))
-    whole = dots + lax.ppermute(dots, "fsdp", swap)
-    back = lax.all_to_all(
-        whole.reshape(experts, 1, LANES), "expert", split_axis=0, concat_axis=0, tiled=True
-    ).reshape(experts, LANES)
+    back = lax.all_to_all(dots, ("fsdp", "expert"), split_axis=0, concat_axis=0, tiled=True)
+    back = back.reshape(2 * experts, LANES)
     other = lax.ppermute(own, "fsdp", swap)
     grad = pl.pallas_call(
         project_kernel,
         out_shape=jax.ShapeDtypeStruct((slots, experts, hidden), BF16),
-        in_specs=[scalar] + [VMEM] * 3,
-        out_specs=VMEM,
+        in_specs=[scalar, VMEM, HBM, HBM],
+        out_specs=HBM,
         scratch_shapes=[
+            pltpu.VMEM((2, width, hidden), BF16),
+            pltpu.VMEM((experts, rows, LANES), BF16),
+            pltpu.VMEM((slots, experts, hidden), BF16),
             pltpu.VMEM((hidden // LANES, (experts + 1) * FULL, LANES), F32),
             pltpu.VMEM((2, hidden // LANES, (experts + 1) * SUB, LANES), F32),
-            pltpu.VMEM(((experts + 1) * FULL, LANES), F32),
-            pltpu.VMEM(((experts + 1) * SUB, LANES), F32),
+            pltpu.VMEM(((experts + 1) * FULL + experts * SUB, LANES), F32),
+            pltpu.SemaphoreType.DMA((5,)),
+            pltpu.SemaphoreType.DMA((slots,)),
         ],
-        compiler_params=PARAMS,
+        compiler_params=MOST,
         cost_estimate=pl.CostEstimate(
             flops=2 * slots * experts * weight.size, bytes_accessed=10 * 1024 * 1024, transcendentals=0
         ),

time: 118 us -> 109 us (0.924)
  local copies, waits for them, and re-layouts: 6.36 us -> 3.74 us
  starting transfers between devices: 43.4 us -> 41.1 us
  waiting for transfers between devices: 45.8 us -> 44.2 us
  Pallas kernels: 20.4 us -> 19.1 us
    all_to_all x1, starting transfers between devices: 9.08 us -> 22.7 us  [on_device(): lax.all_to_all(send, 'expert', split_axis=0, concat_axis=0, tiled=True)]
    ppermute x2, starting transfers between devices: 18.1 us -> 4.92 us  [on_device(): lax.ppermute(lax.dynamic_slice_in_dim(weight, start + first, cut, 0), 'fs...]
    unnamed x12 -> x10, local copies, waits for them, and re-layouts: 6.36 us -> 1.87 us
    all_to_all x1, starting transfers between devices: 10.6 us -> 7.57 us  [on_device(): lax.all_to_all(dots, ('fsdp', 'expert'), split_axis=0, concat_axis=0, til...]
    pallas_call x1, Pallas kernels: 7.15 us -> 4.61 us  [on_device(): pl.pallas_call(align_kernel, out_shape=jax.ShapeDtypeStruct((experts * ro...]
    all_to_all x1, waiting for transfers between devices: 1.87 us -> 4 us  [on_device(): lax.all_to_all(dots, ('fsdp', 'expert'), split_axis=0, concat_axis=0, til...]
    dynamic_slice x0 -> x1, local copies, waits for them, and re-layouts: none -> 1.88 us  [on_device(): lax.dynamic_slice_in_dim(weight, start + first, cut, 0)]
    all_to_all x1, waiting for transfers between devices: 39.9 us -> 38 us  [on_device(): lax.all_to_all(send, 'expert', split_axis=0, concat_axis=0, tiled=True)]
  transfers between devices with their start and end apart: 6 -> 6, of which waited for: 4 -> 3; matrix products, arithmetic and copies ran while one was open for 1% -> 2% of each run, Pallas kernels for 12% -> 11%
where the time goes in v4:
time: 109 us
  waiting for transfers between devices  44.2 us (41%)
  starting transfers between devices  41.1 us (38%)
  Pallas kernels  19.1 us (18%)
  local copies, waits for them, and re-layouts  3.74 us (3%)
    all_to_all x1, waiting for transfers between devices, on_device(): lax.all_to_all(send, 'expert', split_axis=0, concat_axis=0, tiled=True)  38 us
    all_to_all x1, starting transfers between devices, on_device(): lax.all_to_all(send, 'expert', split_axis=0, concat_axis=0, tiled=True)  22.7 us
    all_to_all x1, starting transfers between devices, on_device(): lax.all_to_all(dots, ('fsdp', 'expert'), split_axis=0, concat_axis=0, til...  7.57 us
    pallas_call x1, Pallas kernels, on_device(): pl.pallas_call(project_kernel, out_shape=jax.ShapeDtypeStruct((slots, exp...  7.42 us
    ppermute x2, starting transfers between devices, on_device(): lax.ppermute(lax.dynamic_slice_in_dim(weight, start + first, cut, 0), 'fs...  4.92 us
    pallas_call x1, Pallas kernels, on_device(): pl.pallas_call(align_kernel, out_shape=jax.ShapeDtypeStruct((experts * ro...  4.61 us
    all_to_all x1, waiting for transfers between devices, on_device(): lax.all_to_all(dots, ('fsdp', 'expert'), split_axis=0, concat_axis=0, til...  4 us
    ppermute x1, starting transfers between devices, on_device(): other = lax.ppermute(own, 'fsdp', swap)  3.49 us
  transfers between devices with their start and end apart: 6, of which 3 were waited for; matrix products, arithmetic and copies ran while one was open for 2% of the time, Pallas kernels for 11%

profile of v4, /device:TPU:1, one launch (start us, length us, event | category | flops | bytes accessed | tf_op | source)
XLA Modules:
  0.0 108.9 jit_solution(9970924138042526222)
XLA Ops:
  0.6 3.3 %pack.1 = (bf16[32,240,128]{2,1,0:T(8,128)(2,1)}, f32[32,128]{1,0:T(8,128)}) custom-call(s32[4,128]{1,0:T(4,128)} %bitcast.25, bf16[4,128]{1,0:T(4,128)(2,1)} %bitcast.29, bf16[1440,128]{1,0:T(8,128)(2,1)} %bitcast.27), custom_call_target="tpu_custom_call" | custom-call | tf_op jit(solution)/shard_map/pack/pallas_call | solution.py:311
  4.0 0.0 copy-start.2
  4.0 22.7 %all-to-all-start = ((bf16[32,240,128]{2,1,0:T(8,128)(2,1)}), bf16[32,240,128]{2,1,0:T(8,128)(2,1)S(1)}, u32[]{:S(2)}, u32[]{:S(2)}) async-start(bf16[32,240,128]{2,1,0:T(8,128)(2,1)} %get-tuple-element.11), calls=%async_computation | async-start | bytes 3932160 | tf_op jit(solution)/shard_map/all_to_all | solution.py:331
  26.7 0.0 copy-start.1
  26.7 1.9 %constant_dynamic-slice_fusion = (bf16[720,768]{1,0:T(8,128)(2,1)S(1)}, bf16[720,768]{1,0:T(8,128)(2,1)S(1)}) fusion(bf16[2880,768]{1,0:T(8,128)(2,1)} %bitcast.19, s32[]{:T(128)S(6)} %select_n.7, s32[]{:T(128)S(6)} %select_n.6), kind=kLoop, calls=%fused_computation | loop fusion | bytes 4423688 | tf_op jit(solution)/shard_map/dynamic_slice | solution.py:340
  28.6 3.0 %collective-permute-start.2 = (bf16[720,768]{1,0:T(8,128)(2,1)S(1)}, bf16[720,768]{1,0:T(8,128)(2,1)S(1)}, u32[]{:S(2)}, u32[]{:S(2)}) collective-permute-start(bf16[720,768]{1,0:T(8,128)(2,1)S(1)} %get-tuple-element.18), channel_id=1, source_target_pairs={{0,1},{1,0},{2,3},{3,2},{4,5},{5,4},{6,7},{7,6},{8,9},{9,8},{10,11... | collective-permute-start | bytes 3317768 | tf_op jit(solution)/shard_map/ppermute | solution.py:340
  31.6 1.9 %collective-permute-start.1 = (bf16[720,768]{1,0:T(8,128)(2,1)S(1)}, bf16[720,768]{1,0:T(8,128)(2,1)S(1)}, u32[]{:S(2)}, u32[]{:S(2)}) collective-permute-start(bf16[720,768]{1,0:T(8,128)(2,1)S(1)} %get-tuple-element.19), channel_id=1, source_target_pairs={{0,1},{1,0},{2,3},{3,2},{4,5},{5,4},{6,7},{7,6},{8,9},{9,8},{10,11... | collective-permute-start | bytes 3317768 | tf_op jit(solution)/shard_map/ppermute | solution.py:340
  33.5 2.4 %collective-permute-start = (bf16[20,32,768]{2,1,0:T(8,128)(2,1)S(1)}, bf16[20,32,768]{2,1,0:T(8,128)(2,1)S(1)}, u32[]{:S(2)}, u32[]{:S(2)}) collective-permute-start(bf16[20,32,768]{2,1,0:T(8,128)(2,1)S(1)} %bitcast.22), channel_id=1, source_target_pairs={{0,1},{1,0},{2,3},{3,2},{4,5},{5,4},{6,7},{7,6},{8,9},{9,8},{10,11... | collective-permute-start | bytes 2949128 | tf_op jit(solution)/shard_map/ppermute | solution.py:336
  35.9 2.2 %collective-permute-done.act_other_ref = bf16[20,32,768]{2,1,0:T(8,128)(2,1)S(1)} collective-permute-done((bf16[20,32,768]{2,1,0:T(8,128)(2,1)S(1)}, bf16[20,32,768]{2,1,0:T(8,128)(2,1)S(1)}, u32[]{:S(2)}, u32[]{:S(2)}) %collective-permute-start) | collective-permute-done | bytes 983072 | tf_op jit(solution)/shard_map/ppermute | solution.py:336
  38.1 0.0 collective-permute-done.2.other_high_ref
  38.1 0.0 collective-permute-done.1.other_low_ref
  38.1 4.6 %align.1 = f32[7680,128]{1,0:T(8,128)S(1)} custom-call(s32[1]{0:T(128)} %bitcast.5.core_ref, bf16[20,32,768]{2,1,0:T(8,128)(2,1)S(1)} %bitcast.23, bf16[20,32,768]{2,1,0:T(8,128)(2,1)S(1)} %collective-permute-done.act_other_ref, bf16[2880,768]{1,0:T(8,128)(2,1)S(1)} %bitcast.21, bf16[720,768]{1,0:T(8,128)(2,1)S(1)} %collective-permute-done.1.other_low_ref, ...), custom_call_target="tpu_custom_call" | custom-call | flops 2831155200 | bytes 16777216 | tf_op jit(solution)/shard_map/align/pallas_call | solution.py:343
  42.7 0.0 copy-start
  42.8 1.8 %copy-done = f32[7680,128]{1,0:T(8,128)} copy-done((f32[7680,128]{1,0:T(8,128)}, f32[7680,128]{1,0:T(8,128)S(1)}, u32[]{:S(2)}) %copy-start) | copy-done | bytes 3932184
  44.6 38.0 %all-to-all-done.refs_0_.own_ref = bf16[32,240,128]{2,1,0:T(8,128)(2,1)S(1)} async-done(((bf16[32,240,128]{2,1,0:T(8,128)(2,1)}), bf16[32,240,128]{2,1,0:T(8,128)(2,1)S(1)}, u32[]{:S(2)}, u32[]{:S(2)}) %all-to-all-start) | async-done | bytes 1966112 | tf_op jit(solution)/shard_map/all_to_all | solution.py:331
  82.6 2.9 %dots.1 = f32[64,128]{1,0:T(8,128)} custom-call(bf16[32,240,128]{2,1,0:T(8,128)(2,1)S(1)} %all-to-all-done.refs_0_.own_ref, f32[32,240,128]{2,1,0:T(8,128)} %bitcast.18), custom_call_target="tpu_custom_call" | custom-call | tf_op jit(solution)/shard_map/dots/pallas_call | solution.py:354
  85.6 3.5 %collective-permute-start.3 = (bf16[32,240,128]{2,1,0:T(8,128)(2,1)S(1)}, bf16[32,240,128]{2,1,0:T(8,128)(2,1)}, u32[]{:S(2)}, u32[]{:S(2)}) collective-permute-start(bf16[32,240,128]{2,1,0:T(8,128)(2,1)S(1)} %all-to-all-done.refs_0_.own_ref), channel_id=1, source_target_pairs={{0,1},{1,0},{2,3},{3,2},{4,5},{5,4},{6,7},{7,6},{8,9},{9,8},{10,11... | collective-permute-start | bytes 5898248 | tf_op jit(solution)/shard_map/ppermute | solution.py:369
  89.0 7.6 %all-to-all-start.1 = ((f32[64,1,128]{2,1,0:T(1,128)}), f32[64,1,128]{2,1,0:T(1,128)S(1)}, u32[]{:S(2)}, u32[]{:S(2)}) async-start(f32[64,1,128]{2,1,0:T(1,128)} %bitcast.11), calls=%async_computation.1 | async-start | bytes 65536 | tf_op jit(solution)/shard_map/all_to_all | solution.py:367
  96.6 0.0 copy-start.4
  96.7 0.0 collective-permute-done.3.other_hbm
  96.7 7.4 %project.1 = bf16[20,32,768]{2,1,0:T(8,128)(2,1)} custom-call(s32[1]{0:T(128)} %bitcast.5.core_ref, bf16[32,240,128]{2,1,0:T(8,128)(2,1)S(1)} %all-to-all-done.refs_0_.own_ref, bf16[32,240,128]{2,1,0:T(8,128)(2,1)} %collective-permute-done.3.other_hbm, bf16[2880,768]{1,0:T(8,128)(2,1)} %bitcast.20), custom_call_target="tpu_custom_call" | custom-call | flops 2831155200 | bytes 10485760 | tf_op jit(solution)/shard_map/project/pallas_call | solution.py:370
  104.1 4.0 %all-to-all-done.1 = f32[64,1,128]{2,1,0:T(1,128)S(1)} async-done(((f32[64,1,128]{2,1,0:T(1,128)}), f32[64,1,128]{2,1,0:T(1,128)S(1)}, u32[]{:S(2)}, u32[]{:S(2)}) %all-to-all-start.1) | async-done | bytes 32800 | tf_op jit(solution)/shard_map/all_to_all | solution.py:367
  108.1 0.0 copy-done.4
  108.1 0.8 collect.1
  (4 shorter events, 0.0 us)
Async XLA Ops:
  4.0 29.5 %copy-start.2 = (bf16[1,1,32,20,768]{4,2,3,1,0:T(8,128)(2,1)S(1)}, bf16[1,1,32,20,768]{4,2,3,1,0:T(8,128)(2,1)}, u32[]{:S(2)}) copy-start(bf16[1,1,32,20,768]{4,2,3,1,0:T(8,128)(2,1)} %param.9) | copy-start | bytes 2949124
  4.0 78.6 %all-to-all-start = ((bf16[32,240,128]{2,1,0:T(8,128)(2,1)}), bf16[32,240,128]{2,1,0:T(8,128)(2,1)S(1)}, u32[]{:S(2)}, u32[]{:S(2)}) async-start(bf16[32,240,128]{2,1,0:T(8,128)(2,1)} %get-tuple-element.11), calls=%async_computation | async-start | bytes 3932160 | tf_op jit(solution)/shard_map/all_to_all | solution.py:331
  26.7 11.4 %copy-start.1 = (bf16[1,768,2880]{1,2,0:T(8,128)(2,1)S(1)}, bf16[1,768,2880]{1,2,0:T(8,128)(2,1)}, u32[]{:S(2)}) copy-start(bf16[1,768,2880]{1,2,0:T(8,128)(2,1)} %param.8) | copy-start | bytes 13271044
  28.6 9.5 %collective-permute-start.2 = (bf16[720,768]{1,0:T(8,128)(2,1)S(1)}, bf16[720,768]{1,0:T(8,128)(2,1)S(1)}, u32[]{:S(2)}, u32[]{:S(2)}) collective-permute-start(bf16[720,768]{1,0:T(8,128)(2,1)S(1)} %get-tuple-element.18), channel_id=1, source_target_pairs={{0,1},{1,0},{2,3},{3,2},{4,5},{5,4},{6,7},{7,6},{8,9},{9,8},{10,11... | collective-permute-start | bytes 3317768 | tf_op jit(solution)/shard_map/ppermute | solution.py:340
  31.6 6.5 %collective-permute-start.1 = (bf16[720,768]{1,0:T(8,128)(2,1)S(1)}, bf16[720,768]{1,0:T(8,128)(2,1)S(1)}, u32[]{:S(2)}, u32[]{:S(2)}) collective-permute-start(bf16[720,768]{1,0:T(8,128)(2,1)S(1)} %get-tuple-element.19), channel_id=1, source_target_pairs={{0,1},{1,0},{2,3},{3,2},{4,5},{5,4},{6,7},{7,6},{8,9},{9,8},{10,11... | collective-permute-start | bytes 3317768 | tf_op jit(solution)/shard_map/ppermute | solution.py:340
  33.5 4.6 %collective-permute-start = (bf16[20,32,768]{2,1,0:T(8,128)(2,1)S(1)}, bf16[20,32,768]{2,1,0:T(8,128)(2,1)S(1)}, u32[]{:S(2)}, u32[]{:S(2)}) collective-permute-start(bf16[20,32,768]{2,1,0:T(8,128)(2,1)S(1)} %bitcast.22), channel_id=1, source_target_pairs={{0,1},{1,0},{2,3},{3,2},{4,5},{5,4},{6,7},{7,6},{8,9},{9,8},{10,11... | collective-permute-start | bytes 2949128 | tf_op jit(solution)/shard_map/ppermute | solution.py:336
  42.7 1.9 %copy-start = (f32[7680,128]{1,0:T(8,128)}, f32[7680,128]{1,0:T(8,128)S(1)}, u32[]{:S(2)}) copy-start(f32[7680,128]{1,0:T(8,128)S(1)} %align.1) | copy-start | bytes 11796484
  85.6 11.1 %collective-permute-start.3 = (bf16[32,240,128]{2,1,0:T(8,128)(2,1)S(1)}, bf16[32,240,128]{2,1,0:T(8,128)(2,1)}, u32[]{:S(2)}, u32[]{:S(2)}) collective-permute-start(bf16[32,240,128]{2,1,0:T(8,128)(2,1)S(1)} %all-to-all-done.refs_0_.own_ref), channel_id=1, source_target_pairs={{0,1},{1,0},{2,3},{3,2},{4,5},{5,4},{6,7},{7,6},{8,9},{9,8},{10,11... | collective-permute-start | bytes 5898248 | tf_op jit(solution)/shard_map/ppermute | solution.py:369
  89.0 19.0 %all-to-all-start.1 = ((f32[64,1,128]{2,1,0:T(1,128)}), f32[64,1,128]{2,1,0:T(1,128)S(1)}, u32[]{:S(2)}, u32[]{:S(2)}) async-start(f32[64,1,128]{2,1,0:T(1,128)} %bitcast.11), calls=%async_computation.1 | async-start | bytes 65536 | tf_op jit(solution)/shard_map/all_to_all | solution.py:367
  96.6 11.5 %copy-start.3 = (f32[32,128]{1,0:T(8,128)S(1)}, f32[32,128]{1,0:T(8,128)}, u32[]{:S(2)}) copy-start(f32[32,128]{1,0:T(8,128)} %get-tuple-element.16.refs_1_) | copy-start | bytes 49156
  96.6 11.5 %copy-start.4 = (s32[128,4]{0,1:T(4,128)S(1)}, s32[128,4]{0,1:T(4,128)}, u32[]{:S(2)}) copy-start(s32[128,4]{0,1:T(4,128)} %param.7) | copy-start | bytes 6148

commit v5 on v4

--- a/solution.py
+++ b/solution.py
@@ -60,12 +60,17 @@
 
     inputs[2].wait()
     cot = cot_ref[...]
-    tail = jnp.concatenate(
-        [cot[whole:], jnp.zeros((LANES - (width - whole), tokens), BF16)], axis=0
-    )
-    free = (
-        lax.broadcasted_iota(jnp.int32, (LANES, tokens), 0) >= width - whole
-    ).astype(F32).astype(BF16)
+    extra = width - whole
+    groups = LANES // extra
+    lane = lax.broadcasted_iota(jnp.int32, (LANES, tokens), 0)
+
+    def blank(count):
+        return [jnp.zeros((count, tokens), BF16)] if count else []
+
+    padded = [
+        jnp.concatenate(blank(g * extra) + [cot[whole:]] + blank(LANES - (g + 1) * extra), axis=0)
+        for g in range(groups)
+    ]
 
     def pick(rows, columns):
         return lax.dot_general(rows, columns, NT, preferred_element_type=F32)
@@ -88,25 +93,32 @@
             gated.reshape(experts * count, tokens).astype(BF16),
         )
 
-    rows_a, gated_a = select(FULL, lambda r: r)
+    rows_a, _ = select(FULL, lambda r: r)
     for b in range(blocks - 1):
         put(b * FULL, FULL, pick(rows_a, cot[b * LANES : (b + 1) * LANES]))
         ship(b * FULL, FULL)
-    put((blocks - 1) * FULL, FULL, pick(rows_a, tail) + pick(gated_a, free))
-    ship((blocks - 1) * FULL, FULL)
-
-    base = blocks * FULL
-    rows_l, _ = select(SUB, lambda r: jnp.where(r < SUB // 2, r + FULL, -2))
-    rows_h, gated_h = select(SUB, lambda r: jnp.where(r < SUB // 2, -2, r + FULL - SUB // 2))
+
+    base = (blocks - 1) * FULL
+    quarter = SUB // 2
+    rows_l, _ = select(SUB, lambda r: jnp.where(r < quarter, r + FULL, -2))
+    rows_h, _ = select(SUB, lambda r: jnp.where(r < quarter, -2, r + FULL - quarter))
     for b in range(half):
-        low = pick(rows_l, cot[b * LANES : (b + 1) * LANES])
+        value = pick(rows_l, cot[b * LANES : (b + 1) * LANES])
         if half + b < blocks - 1:
-            high = pick(rows_h, cot[(half + b) * LANES : (half + b + 1) * LANES])
+            value += pick(rows_h, cot[(half + b) * LANES : (half + b + 1) * LANES])
         else:
-            high = pick(rows_h, tail) + pick(gated_h, free)
-        put(base + b * SUB, SUB, low + high)
+            for g in range(groups):
+                rows_g, _ = select(SUB, lambda r: jnp.where(r < quarter, -2, r + (g - 1) * quarter))
+                value += pick(rows_g, padded[g])
+        put(base + b * SUB, SUB, value)
         if b % 2:
             ship(base + (b - 1) * SUB, 2 * SUB)
+    value = pick(rows_l, padded[0])
+    for i in range(3):
+        _, gated = select(SUB, lambda r: r + i * SUB)
+        value += pick(gated, (lane == extra + i).astype(F32).astype(BF16))
+    put(base + half * SUB, SUB, value)
+    ship(base + half * SUB, SUB)
     for copy in outputs:
         copy.wait()
 
@@ -119,32 +131,69 @@
     rows = out_ref.shape[0] // sources
     start = core_ref[0] * width
     acts = [ref[...].reshape(slots * sources, hidden) for ref in (act_ref, act_other_ref)]
-    for first in range(0, blocks, 2):
-        at, count = first * LANES, min(2 * LANES, width - first * LANES)
-        out = jnp.zeros((slots * sources, 2 * LANES), F32)
-        for c, act in enumerate(acts):
-            if c:
-                cut = other_low_ref.shape[0]
-                columns = [other_low_ref[at : at + count, :]] if at < cut else []
-                if at + count > cut:
-                    columns.append(other_high_ref[max(at - cut, 0) : at + count - cut, :])
-                columns = jnp.concatenate(columns, axis=0)
-            else:
-                columns = weight_ref[pl.ds(pl.multiple_of(start + at, 16), count), :]
-            if count < 2 * LANES:
-                columns = jnp.concatenate(
-                    [columns, jnp.zeros((2 * LANES - count, hidden), BF16)], axis=0
-                )
-            out = out + lax.dot_general(act, columns, NT, preferred_element_type=F32)
-        for b in (first, first + 1):
+    whole = width // LANES * LANES
+    extra = width - whole
+    quarter = SUB // 2
+    base = (blocks - 1) * FULL
+
+    def columns_of(at, count):
+        cut = other_low_ref.shape[0]
+        other = [other_low_ref[at : at + count, :]] if at < cut else []
+        if at + count > cut:
+            other.append(other_high_ref[max(at - cut, 0) : at + count - cut, :])
+        return (
+            weight_ref[pl.ds(pl.multiple_of(start + at, 16), count), :],
+            jnp.concatenate(other, axis=0),
+        )
+
+    def store(row, value):
+        out_ref[pl.ds(row, sources, stride=rows), :] = value
+
+    def slot(value, s, n=0):
+        return value[s * sources : (s + 1) * sources, n * LANES : (n + 1) * LANES]
+
+    for first in range(0, blocks - 1, 2):
+        at, count = first * LANES, min(2 * LANES, whole - first * LANES)
+        out = sum(
+            lax.dot_general(act, columns, NT, preferred_element_type=F32)
+            for act, columns in zip(acts, columns_of(at, count))
+        )
+        for b in range(first, first + count // LANES):
             for s in range(slots):
                 if s < FULL:
                     row = b * FULL + s
                 else:
-                    row = blocks * FULL + b % half * SUB + b // half * (SUB // 2) + s - FULL
-                out_ref[pl.ds(row, sources, stride=rows), :] = out[
-                    s * sources : (s + 1) * sources, (b - first) * LANES : (b - first + 1) * LANES
-                ]
+                    row = base + b % half * SUB + b // half * quarter + s - FULL
+                store(row, slot(out, s, b - first))
+
+    last = columns_of(whole, extra)
+    blank = jnp.zeros((extra, hidden), BF16)
+    tails = []
+    for g in range(LANES // extra):
+        padded = [
+            jnp.concatenate([x if i == g else blank for i in range(LANES // extra)], axis=0) for x in last
+        ]
+        tails.append(
+            sum(
+                lax.dot_general(
+                    act[g * quarter * sources : (g + 1) * quarter * sources],
+                    columns,
+                    NT,
+                    preferred_element_type=F32,
+                )
+                for act, columns in zip(acts, padded)
+            )
+        )
+        if g == 0:
+            few = sum(
+                lax.dot_general(act[FULL * sources :], columns, NT, preferred_element_type=F32)
+                for act, columns in zip(acts, padded)
+            )
+    packed = sum(tails)
+    for s in range(quarter):
+        store(base + (half - 1) * SUB + quarter + s, slot(packed, s))
+        store(base + half * SUB + s, slot(few, s))
+        store(base + half * SUB + quarter + s, jnp.zeros((sources, LANES), F32))
 
 
 def dots_kernel(blocks, rows_ref, aligned_hbm, dots_ref, aligned_ref, sems):
@@ -160,33 +209,47 @@
     for copy in copies:
         copy.start()
 
-    def reduce(p, first, count, steps):
-        total = jnp.zeros((step, count, LANES), F32)
-        of = slice(p * step, (p + 1) * step)
-        for b in range(steps):
-            at = slice(first + b * count, first + (b + 1) * count)
-            total = total + rows_ref[of, at, :].astype(F32) * aligned_ref[of, at, :]
-        return jnp.sum(total, axis=2, keepdims=True)
+    quarter = SUB // 2
+    half = blocks // 2
+    base = (blocks - 1) * FULL
+    extra = LANES // (FULL // quarter)
+
+    def times(p, first, count):
+        of, at = slice(p * step, (p + 1) * step), slice(first, first + count)
+        return rows_ref[of, at, :].astype(F32) * aligned_ref[of, at, :]
 
     def spread(value, count, slot):
         lane = lax.broadcasted_iota(jnp.int32, (step, count, LANES), 2)
         row = lax.broadcasted_iota(jnp.int32, (step, count, LANES), 1)
+        value = jnp.sum(value, axis=2, keepdims=True)
         return jnp.sum(jnp.where(lane == slot(row), value, 0.0), axis=1)
 
+    lane = lax.broadcasted_iota(jnp.int32, (step, SUB, LANES), 2)
+    row = lax.broadcasted_iota(jnp.int32, (step, SUB, LANES), 1)
     for p in range(parts):
         copies[p].wait()
-        full = spread(reduce(p, 0, FULL, blocks), FULL, lambda r: r)
-        split = spread(
-            reduce(p, blocks * FULL, SUB, blocks // 2),
-            SUB,
-            lambda r: jnp.where(r < SUB // 2, r, r - SUB // 2) + FULL,
-        )
+        total = times(p, 0, FULL)
+        for b in range(1, blocks - 1):
+            total = total + times(p, b * FULL, FULL)
+        dots = spread(total, FULL, lambda r: r)
+        mixed = times(p, base + (half - 1) * SUB, SUB)
+        total = times(p, base + half * SUB, SUB) + jnp.where(row < quarter, mixed, 0.0)
+        for b in range(half - 1):
+            total = total + times(p, base + b * SUB, SUB)
+        dots = dots + spread(total, SUB, lambda r: jnp.where(r < quarter, r, r - quarter) + FULL)
+        for g in range(FULL // quarter):
+            here = (lane >= g * extra) & (lane < (g + 1) * extra)
+            dots = dots + spread(
+                jnp.where(here, mixed, 0.0),
+                SUB,
+                lambda r: jnp.where(r < quarter, -1, r + (g - 1) * quarter),
+            )
         for first in (p * step, sources + p * step):
-            dots_ref[first : first + step, :] = full + split
+            dots_ref[first : first + step, :] = dots
 
 
 def project_kernel(
-    core_ref, own_ref, other_hbm, weight_hbm, grad_hbm, weight_ref, other_ref, grad_ref, part, tails, gates, in_sems, out_sems
+    core_ref, own_ref, other_hbm, weight_hbm, grad_hbm, weight_ref, other_ref, grad_ref, part, tails, ends, gates, in_sems, out_sems
 ):
     sources = own_ref.shape[0]
     _, width, hidden = weight_ref.shape
@@ -195,7 +258,10 @@
     blocks = -(-width // LANES)
     half = blocks // 2
     tail = width % LANES
-    base = blocks * FULL
+    base = (blocks - 1) * FULL
+    quarter = SUB // 2
+    few = sources * SUB
+    groups = LANES // tail
     split = sources * FULL
     mine = core_ref[0] * width
 
@@ -223,21 +289,20 @@
         return slice(n * LANES, (n + 1) * LANES)
 
     def product(ref, c, h):
-        last = width - cut if h else cut
+        steps = blocks - 1 - half if h else half
 
         def dot(first, count):
-            rows = [block(ref, first + b * count, count) for b in range(half)]
+            rows = [block(ref, first + b * count, count) for b in range(steps)]
             return lax.dot_general(
-                jnp.concatenate(rows, axis=1)[:, :last],
-                weight_ref[c, h * cut : h * cut + last, :],
+                jnp.concatenate(rows, axis=1),
+                weight_ref[c, h * cut : h * cut + steps * LANES, :],
                 NN,
                 preferred_element_type=F32,
             )
 
         return dot(h * half * FULL, FULL), dot(base, SUB)
 
-    gates[:split] = block(own_ref, (blocks - 1) * FULL, FULL).astype(F32)
-    gates[split : split + sources * SUB] = block(own_ref, base + (half - 1) * SUB, SUB).astype(F32)
+    gates[:few] = block(own_ref, base + half * SUB, SUB).astype(F32)
     for c, ref in enumerate((own_ref, other_ref)):
         for h in (0, 1):
             if c == 1 and h == 0:
@@ -246,24 +311,44 @@
             out, some = product(ref, c, h)
             for n in range(columns):
                 full = out[:, lanes(n)]
-                few = some[:, lanes(n)]
+                rest = some[:, lanes(n)]
                 if c or h:
                     full = full + part[n, :split]
                 if c:
-                    few = few + tails[h, n, : sources * SUB]
+                    rest = rest + tails[h, n, :few]
                 part[n, :split] = full
-                tails[h, n, : sources * SUB] = few
+                tails[h, n, :few] = rest
+    lane = lax.broadcasted_iota(jnp.int32, (1, LANES), 1)
+    mixed, last = [
+        [block(ref, base + at * SUB, SUB) for ref in (own_ref, other_ref)] for at in (half - 1, half)
+    ]
+    rows = []
+    for g in range(groups + 1):
+        first = g % groups * tail
+        keep = ((lane >= first) & (lane < first + tail)).astype(F32).astype(BF16)
+        rows.append(jnp.concatenate([x * keep for x in (mixed if g < groups else last)], axis=1))
+    out = lax.dot_general(
+        jnp.concatenate(rows, axis=0),
+        jnp.concatenate([weight_ref[c, width - tail :, :] for c in (0, 1) for _ in range(groups)], axis=0),
+        NN,
+        preferred_element_type=F32,
+    )
+    for n in range(columns):
+        for g in range(groups):
+            ends[g, n, :few] = out[g * few : (g + 1) * few, lanes(n)]
+        tails[0, n, :few] += out[groups * few :, lanes(n)]
 
     outputs = []
     for s in range(slots):
-        if s < FULL:
-            gate = gates[pl.ds(s, sources, stride=FULL), :]
-        else:
-            gate = gates[pl.ds(split + s - FULL + SUB // 2, sources, stride=SUB), :]
-        gate = jnp.broadcast_to(gate[:, tail : tail + 1], (sources, LANES))
+        gate = gates[pl.ds(s % SUB, sources, stride=SUB), :]
+        at = tail + s // SUB
+        gate = jnp.broadcast_to(gate[:, at : at + 1], (sources, LANES))
         for n in range(columns):
             if s < FULL:
-                proj = part[n, pl.ds(s, sources, stride=FULL), :]
+                proj = (
+                    part[n, pl.ds(s, sources, stride=FULL), :]
+                    + ends[s // quarter, n, pl.ds(quarter + s % quarter, sources, stride=SUB), :]
+                )
             else:
                 proj = (
                     tails[0, n, pl.ds(s - FULL, sources, stride=SUB), :]
@@ -306,7 +391,7 @@
     topk = expert_ids.shape[1]
     _, _, _, slots, hidden = hidden_act.shape
     blocks = -(-width // LANES)
-    rows = blocks * FULL + blocks // 2 * SUB
+    rows = (blocks - 1) * FULL + (blocks // 2 + 1) * SUB
     ids = expert_ids.T
     send, rank = pl.pallas_call(
         pack_kernel,
@@ -378,7 +463,8 @@
             pltpu.VMEM((slots, experts, hidden), BF16),
             pltpu.VMEM((hidden // LANES, (experts + 1) * FULL, LANES), F32),
             pltpu.VMEM((2, hidden // LANES, (experts + 1) * SUB, LANES), F32),
-            pltpu.VMEM(((experts + 1) * FULL + experts * SUB, LANES), F32),
+            pltpu.VMEM((LANES // (width % LANES), hidden // LANES, (experts + 1) * SUB, LANES), F32),
+            pltpu.VMEM(((experts + 1) * SUB, LANES), F32),
             pltpu.SemaphoreType.DMA((5,)),
             pltpu.SemaphoreType.DMA((slots,)),
         ],

time: 109 us -> 109 us (level)
  no operation moved by 1% of the time
where the time goes in v5:
time: 109 us; the launch traced here: 108 us
  waiting for transfers between devices  43.5 us (40%)
  starting transfers between devices  41.2 us (38%)
  Pallas kernels  18.9 us (17%)
  local copies, waits for them, and re-layouts  3.73 us (3%)
    all_to_all x1, waiting for transfers between devices, on_device(): lax.all_to_all(send, 'expert', split_axis=0, concat_axis=0, tiled=True)  37.9 us
    all_to_all x1, starting transfers between devices, on_device(): lax.all_to_all(send, 'expert', split_axis=0, concat_axis=0, tiled=True)  22.7 us
    pallas_call x1, Pallas kernels, on_device(): pl.pallas_call(project_kernel, out_shape=jax.ShapeDtypeStruct((slots, exp...  7.98 us
    all_to_all x1, starting transfers between devices, on_device(): lax.all_to_all(dots, ('fsdp', 'expert'), split_axis=0, concat_axis=0, til...  7.61 us
    ppermute x2, starting transfers between devices, on_device(): lax.ppermute(lax.dynamic_slice_in_dim(weight, start + first, cut, 0), 'fs...  4.91 us
    pallas_call x1, Pallas kernels, on_device(): pl.pallas_call(align_kernel, out_shape=jax.ShapeDtypeStruct((experts * ro...  3.84 us
    ppermute x1, starting transfers between devices, on_device(): other = lax.ppermute(own, 'fsdp', swap)  3.6 us
    all_to_all x1, waiting for transfers between devices, on_device(): lax.all_to_all(dots, ('fsdp', 'expert'), split_axis=0, concat_axis=0, til...  3.45 us
  transfers between devices with their start and end apart: 6, of which 3 were waited for; matrix products, arithmetic and copies ran while one was open for 2% of the time, Pallas kernels for 11%

profile of v5, /device:TPU:1, one launch (start us, length us, event | category | flops | bytes accessed | tf_op | source)
XLA Modules:
  0.0 108.2 jit_solution(1485697993347925707)
XLA Ops:
  0.6 3.4 %pack.1 = (bf16[32,232,128]{2,1,0:T(8,128)(2,1)}, f32[32,128]{1,0:T(8,128)}) custom-call(s32[4,128]{1,0:T(4,128)} %bitcast.25, bf16[4,128]{1,0:T(4,128)(2,1)} %bitcast.29, bf16[1440,128]{1,0:T(8,128)(2,1)} %bitcast.27), custom_call_target="tpu_custom_call" | custom-call | tf_op jit(solution)/shard_map/pack/pallas_call | solution.py:396
  4.0 0.0 copy-start.2
  4.1 22.7 %all-to-all-start = ((bf16[32,232,128]{2,1,0:T(8,128)(2,1)}), bf16[32,232,128]{2,1,0:T(8,128)(2,1)S(1)}, u32[]{:S(2)}, u32[]{:S(2)}) async-start(bf16[32,232,128]{2,1,0:T(8,128)(2,1)} %get-tuple-element.11), calls=%async_computation | async-start | bytes 3801088 | tf_op jit(solution)/shard_map/all_to_all | solution.py:416
  26.8 0.0 copy-start.1
  26.8 1.9 %constant_dynamic-slice_fusion = (bf16[720,768]{1,0:T(8,128)(2,1)S(1)}, bf16[720,768]{1,0:T(8,128)(2,1)S(1)}) fusion(bf16[2880,768]{1,0:T(8,128)(2,1)} %bitcast.19, s32[]{:T(128)S(6)} %select_n.7, s32[]{:T(128)S(6)} %select_n.6), kind=kLoop, calls=%fused_computation | loop fusion | bytes 4423688 | tf_op jit(solution)/shard_map/dynamic_slice | solution.py:425
  28.7 3.0 %collective-permute-start.2 = (bf16[720,768]{1,0:T(8,128)(2,1)S(1)}, bf16[720,768]{1,0:T(8,128)(2,1)S(1)}, u32[]{:S(2)}, u32[]{:S(2)}) collective-permute-start(bf16[720,768]{1,0:T(8,128)(2,1)S(1)} %get-tuple-element.18), channel_id=1, source_target_pairs={{0,1},{1,0},{2,3},{3,2},{4,5},{5,4},{6,7},{7,6},{8,9},{9,8},{10,11... | collective-permute-start | bytes 3317768 | tf_op jit(solution)/shard_map/ppermute | solution.py:425
  31.7 1.9 %collective-permute-start.1 = (bf16[720,768]{1,0:T(8,128)(2,1)S(1)}, bf16[720,768]{1,0:T(8,128)(2,1)S(1)}, u32[]{:S(2)}, u32[]{:S(2)}) collective-permute-start(bf16[720,768]{1,0:T(8,128)(2,1)S(1)} %get-tuple-element.19), channel_id=1, source_target_pairs={{0,1},{1,0},{2,3},{3,2},{4,5},{5,4},{6,7},{7,6},{8,9},{9,8},{10,11... | collective-permute-start | bytes 3317768 | tf_op jit(solution)/shard_map/ppermute | solution.py:425
  33.6 0.0 copy-done.2
  33.6 2.4 %collective-permute-start = (bf16[20,32,768]{2,1,0:T(8,128)(2,1)S(1)}, bf16[20,32,768]{2,1,0:T(8,128)(2,1)S(1)}, u32[]{:S(2)}, u32[]{:S(2)}) collective-permute-start(bf16[20,32,768]{2,1,0:T(8,128)(2,1)S(1)} %bitcast.22), channel_id=1, source_target_pairs={{0,1},{1,0},{2,3},{3,2},{4,5},{5,4},{6,7},{7,6},{8,9},{9,8},{10,11... | collective-permute-start | bytes 2949128 | tf_op jit(solution)/shard_map/ppermute | solution.py:421
  36.0 2.2 %collective-permute-done.act_other_ref = bf16[20,32,768]{2,1,0:T(8,128)(2,1)S(1)} collective-permute-done((bf16[20,32,768]{2,1,0:T(8,128)(2,1)S(1)}, bf16[20,32,768]{2,1,0:T(8,128)(2,1)S(1)}, u32[]{:S(2)}, u32[]{:S(2)}) %collective-permute-start) | collective-permute-done | bytes 983072 | tf_op jit(solution)/shard_map/ppermute | solution.py:421
  38.2 0.0 collective-permute-done.2.other_high_ref
  38.2 0.0 collective-permute-done.1.other_low_ref
  38.2 0.0 copy-done.1
  38.2 3.8 %align.1 = f32[7424,128]{1,0:T(8,128)S(1)} custom-call(s32[1]{0:T(128)} %bitcast.5.core_ref, bf16[20,32,768]{2,1,0:T(8,128)(2,1)S(1)} %bitcast.23, bf16[20,32,768]{2,1,0:T(8,128)(2,1)S(1)} %collective-permute-done.act_other_ref, bf16[2880,768]{1,0:T(8,128)(2,1)S(1)} %bitcast.21, bf16[720,768]{1,0:T(8,128)(2,1)S(1)} %collective-permute-done.1.other_low_ref, ...), custom_call_target="tpu_custom_call" | custom-call | flops 2831155200 | bytes 16777216 | tf_op jit(solution)/shard_map/align/pallas_call | solution.py:428
  42.1 1.8 %copy-done = f32[7424,128]{1,0:T(8,128)} copy-done((f32[7424,128]{1,0:T(8,128)}, f32[7424,128]{1,0:T(8,128)S(1)}, u32[]{:S(2)}) %copy-start) | copy-done | bytes 3801112
  43.9 37.9 %all-to-all-done.refs_0_.own_ref = bf16[32,232,128]{2,1,0:T(8,128)(2,1)S(1)} async-done(((bf16[32,232,128]{2,1,0:T(8,128)(2,1)}), bf16[32,232,128]{2,1,0:T(8,128)(2,1)S(1)}, u32[]{:S(2)}, u32[]{:S(2)}) %all-to-all-start) | async-done | bytes 1900576 | tf_op jit(solution)/shard_map/all_to_all | solution.py:416
  81.8 2.9 %dots.1 = f32[64,128]{1,0:T(8,128)} custom-call(bf16[32,232,128]{2,1,0:T(8,128)(2,1)S(1)} %all-to-all-done.refs_0_.own_ref, f32[32,232,128]{2,1,0:T(8,128)} %bitcast.18), custom_call_target="tpu_custom_call" | custom-call | tf_op jit(solution)/shard_map/dots/pallas_call | solution.py:439
  84.7 3.6 %collective-permute-start.3 = (bf16[32,232,128]{2,1,0:T(8,128)(2,1)S(1)}, bf16[32,232,128]{2,1,0:T(8,128)(2,1)}, u32[]{:S(2)}, u32[]{:S(2)}) collective-permute-start(bf16[32,232,128]{2,1,0:T(8,128)(2,1)S(1)} %all-to-all-done.refs_0_.own_ref), channel_id=1, source_target_pairs={{0,1},{1,0},{2,3},{3,2},{4,5},{5,4},{6,7},{7,6},{8,9},{9,8},{10,11... | collective-permute-start | bytes 5701640 | tf_op jit(solution)/shard_map/ppermute | solution.py:454
  88.3 7.6 %all-to-all-start.1 = ((f32[64,1,128]{2,1,0:T(1,128)}), f32[64,1,128]{2,1,0:T(1,128)S(1)}, u32[]{:S(2)}, u32[]{:S(2)}) async-start(f32[64,1,128]{2,1,0:T(1,128)} %bitcast.11), calls=%async_computation.1 | async-start | bytes 65536 | tf_op jit(solution)/shard_map/all_to_all | solution.py:452
  95.9 0.0 copy-start.4
  95.9 0.0 collective-permute-done.3.other_hbm
  95.9 8.0 %project.1 = bf16[20,32,768]{2,1,0:T(8,128)(2,1)} custom-call(s32[1]{0:T(128)} %bitcast.5.core_ref, bf16[32,232,128]{2,1,0:T(8,128)(2,1)S(1)} %all-to-all-done.refs_0_.own_ref, bf16[32,232,128]{2,1,0:T(8,128)(2,1)} %collective-permute-done.3.other_hbm, bf16[2880,768]{1,0:T(8,128)(2,1)} %bitcast.20), custom_call_target="tpu_custom_call" | custom-call | flops 2831155200 | bytes 10485760 | tf_op jit(solution)/shard_map/project/pallas_call | solution.py:455
  103.9 3.5 %all-to-all-done.1 = f32[64,1,128]{2,1,0:T(1,128)S(1)} async-done(((f32[64,1,128]{2,1,0:T(1,128)}), f32[64,1,128]{2,1,0:T(1,128)S(1)}, u32[]{:S(2)}, u32[]{:S(2)}) %all-to-all-start.1) | async-done | bytes 32800 | tf_op jit(solution)/shard_map/all_to_all | solution.py:452
  107.4 0.8 collect.1
  (4 shorter events, 0.0 us)
Async XLA Ops:
  4.0 29.5 %copy-start.2 = (bf16[1,1,32,20,768]{4,2,3,1,0:T(8,128)(2,1)S(1)}, bf16[1,1,32,20,768]{4,2,3,1,0:T(8,128)(2,1)}, u32[]{:S(2)}) copy-start(bf16[1,1,32,20,768]{4,2,3,1,0:T(8,128)(2,1)} %param.9) | copy-start | bytes 2949124
  4.1 77.7 %all-to-all-start = ((bf16[32,232,128]{2,1,0:T(8,128)(2,1)}), bf16[32,232,128]{2,1,0:T(8,128)(2,1)S(1)}, u32[]{:S(2)}, u32[]{:S(2)}) async-start(bf16[32,232,128]{2,1,0:T(8,128)(2,1)} %get-tuple-element.11), calls=%async_computation | async-start | bytes 3801088 | tf_op jit(solution)/shard_map/all_to_all | solution.py:416
  26.8 11.4 %copy-start.1 = (bf16[1,768,2880]{1,2,0:T(8,128)(2,1)S(1)}, bf16[1,768,2880]{1,2,0:T(8,128)(2,1)}, u32[]{:S(2)}) copy-start(bf16[1,768,2880]{1,2,0:T(8,128)(2,1)} %param.8) | copy-start | bytes 13271044
  28.7 9.5 %collective-permute-start.2 = (bf16[720,768]{1,0:T(8,128)(2,1)S(1)}, bf16[720,768]{1,0:T(8,128)(2,1)S(1)}, u32[]{:S(2)}, u32[]{:S(2)}) collective-permute-start(bf16[720,768]{1,0:T(8,128)(2,1)S(1)} %get-tuple-element.18), channel_id=1, source_target_pairs={{0,1},{1,0},{2,3},{3,2},{4,5},{5,4},{6,7},{7,6},{8,9},{9,8},{10,11... | collective-permute-start | bytes 3317768 | tf_op jit(solution)/shard_map/ppermute | solution.py:425
  31.7 6.5 %collective-permute-start.1 = (bf16[720,768]{1,0:T(8,128)(2,1)S(1)}, bf16[720,768]{1,0:T(8,128)(2,1)S(1)}, u32[]{:S(2)}, u32[]{:S(2)}) collective-permute-start(bf16[720,768]{1,0:T(8,128)(2,1)S(1)} %get-tuple-element.19), channel_id=1, source_target_pairs={{0,1},{1,0},{2,3},{3,2},{4,5},{5,4},{6,7},{7,6},{8,9},{9,8},{10,11... | collective-permute-start | bytes 3317768 | tf_op jit(solution)/shard_map/ppermute | solution.py:425
  33.6 4.6 %collective-permute-start = (bf16[20,32,768]{2,1,0:T(8,128)(2,1)S(1)}, bf16[20,32,768]{2,1,0:T(8,128)(2,1)S(1)}, u32[]{:S(2)}, u32[]{:S(2)}) collective-permute-start(bf16[20,32,768]{2,1,0:T(8,128)(2,1)S(1)} %bitcast.22), channel_id=1, source_target_pairs={{0,1},{1,0},{2,3},{3,2},{4,5},{5,4},{6,7},{7,6},{8,9},{9,8},{10,11... | collective-permute-start | bytes 2949128 | tf_op jit(solution)/shard_map/ppermute | solution.py:421
  42.0 1.8 %copy-start = (f32[7424,128]{1,0:T(8,128)}, f32[7424,128]{1,0:T(8,128)S(1)}, u32[]{:S(2)}) copy-start(f32[7424,128]{1,0:T(8,128)S(1)} %align.1) | copy-start | bytes 11403268
  84.7 11.3 %collective-permute-start.3 = (bf16[32,232,128]{2,1,0:T(8,128)(2,1)S(1)}, bf16[32,232,128]{2,1,0:T(8,128)(2,1)}, u32[]{:S(2)}, u32[]{:S(2)}) collective-permute-start(bf16[32,232,128]{2,1,0:T(8,128)(2,1)S(1)} %all-to-all-done.refs_0_.own_ref), channel_id=1, source_target_pairs={{0,1},{1,0},{2,3},{3,2},{4,5},{5,4},{6,7},{7,6},{8,9},{9,8},{10,11... | collective-permute-start | bytes 5701640 | tf_op jit(solution)/shard_map/ppermute | solution.py:454
  88.3 19.1 %all-to-all-start.1 = ((f32[64,1,128]{2,1,0:T(1,128)}), f32[64,1,128]{2,1,0:T(1,128)S(1)}, u32[]{:S(2)}, u32[]{:S(2)}) async-start(f32[64,1,128]{2,1,0:T(1,128)} %bitcast.11), calls=%async_computation.1 | async-start | bytes 65536 | tf_op jit(solution)/shard_map/all_to_all | solution.py:452
  95.9 11.5 %copy-start.3 = (f32[32,128]{1,0:T(8,128)S(1)}, f32[32,128]{1,0:T(8,128)}, u32[]{:S(2)}) copy-start(f32[32,128]{1,0:T(8,128)} %get-tuple-element.16.refs_1_) | copy-start | bytes 49156
  95.9 11.5 %copy-start.4 = (s32[128,4]{0,1:T(4,128)S(1)}, s32[128,4]{0,1:T(4,128)}, u32[]{:S(2)}) copy-start(s32[128,4]{0,1:T(4,128)} %param.7) | copy-start | bytes 6148

commit v6 on v5

--- a/solution.py
+++ b/solution.py
@@ -244,8 +244,8 @@
                 SUB,
                 lambda r: jnp.where(r < quarter, -1, r + (g - 1) * quarter),
             )
-        for first in (p * step, sources + p * step):
-            dots_ref[first : first + step, :] = dots
+        for core in (0, 1):
+            dots_ref[pl.ds(2 * p * step + core, step, stride=2), :] = dots
 
 
 def project_kernel(
@@ -365,7 +365,7 @@
 def collect_kernel(slots, ids_ref, rank_ref, mine_ref, out_ref):
     experts, tokens = rank_ref.shape
     rank = rank_ref[...]
-    back = mine_ref[:experts, :] + mine_ref[experts:, :]
+    back = mine_ref[pl.ds(0, experts, stride=2), :] + mine_ref[pl.ds(1, experts, stride=2), :]
     found = jnp.zeros((experts, tokens), F32)
     for s in range(slots):
         found = jnp.where(rank == float(s), back[:, s : s + 1], found)
@@ -449,7 +449,7 @@
         name="dots",
     )(own, both).reshape(2 * experts, 1, LANES)
     own, dots = lax.optimization_barrier((own, dots))
-    back = lax.all_to_all(dots, ("fsdp", "expert"), split_axis=0, concat_axis=0, tiled=True)
+    back = lax.all_to_all(dots, ("expert", "fsdp"), split_axis=0, concat_axis=0, tiled=True)
     back = back.reshape(2 * experts, LANES)
     other = lax.ppermute(own, "fsdp", swap)
     grad = pl.pallas_call(

time: 109 us -> 109 us (level)
  no operation moved by 1% of the time
where the time goes in v6:
time: 109 us; the launch traced here: 108 us
  waiting for transfers between devices  43.8 us (40%)
  starting transfers between devices  41.1 us (38%)
  Pallas kernels  18.9 us (17%)
  local copies, waits for them, and re-layouts  3.73 us (3%)
    all_to_all x1, waiting for transfers between devices, on_device(): lax.all_to_all(send, 'expert', split_axis=0, concat_axis=0, tiled=True)  37.9 us
    all_to_all x1, starting transfers between devices, on_device(): lax.all_to_all(send, 'expert', split_axis=0, concat_axis=0, tiled=True)  22.7 us
    pallas_call x1, Pallas kernels, on_device(): pl.pallas_call(project_kernel, out_shape=jax.ShapeDtypeStruct((slots, exp...  7.98 us
    all_to_all x1, starting transfers between devices, on_device(): lax.all_to_all(dots, ('expert', 'fsdp'), split_axis=0, concat_axis=0, til...  7.51 us
    ppermute x2, starting transfers between devices, on_device(): lax.ppermute(lax.dynamic_slice_in_dim(weight, start + first, cut, 0), 'fs...  4.91 us
    pallas_call x1, Pallas kernels, on_device(): pl.pallas_call(align_kernel, out_shape=jax.ShapeDtypeStruct((experts * ro...  3.84 us
    all_to_all x1, waiting for transfers between devices, on_device(): lax.all_to_all(dots, ('expert', 'fsdp'), split_axis=0, concat_axis=0, til...  3.73 us
    ppermute x1, starting transfers between devices, on_device(): other = lax.ppermute(own, 'fsdp', swap)  3.6 us
  transfers between devices with their start and end apart: 6, of which 3 were waited for; matrix products, arithmetic and copies ran while one was open for 2% of the time, Pallas kernels for 11%

profile of v6, /device:TPU:1, one launch (start us, length us, event | category | flops | bytes accessed | tf_op | source)
XLA Modules:
  0.0 108.3 jit_solution(783125928768202185)
XLA Ops:
  0.6 3.4 %pack.1 = (bf16[32,232,128]{2,1,0:T(8,128)(2,1)}, f32[32,128]{1,0:T(8,128)}) custom-call(s32[4,128]{1,0:T(4,128)} %bitcast.25, bf16[4,128]{1,0:T(4,128)(2,1)} %bitcast.29, bf16[1440,128]{1,0:T(8,128)(2,1)} %bitcast.27), custom_call_target="tpu_custom_call" | custom-call | tf_op jit(solution)/shard_map/pack/pallas_call | solution.py:396
  4.0 0.0 copy-start.2
  4.1 22.7 %all-to-all-start = ((bf16[32,232,128]{2,1,0:T(8,128)(2,1)}), bf16[32,232,128]{2,1,0:T(8,128)(2,1)S(1)}, u32[]{:S(2)}, u32[]{:S(2)}) async-start(bf16[32,232,128]{2,1,0:T(8,128)(2,1)} %get-tuple-element.11), calls=%async_computation | async-start | bytes 3801088 | tf_op jit(solution)/shard_map/all_to_all | solution.py:416
  26.8 0.0 copy-start.1
  26.8 1.9 %constant_dynamic-slice_fusion = (bf16[720,768]{1,0:T(8,128)(2,1)S(1)}, bf16[720,768]{1,0:T(8,128)(2,1)S(1)}) fusion(bf16[2880,768]{1,0:T(8,128)(2,1)} %bitcast.19, s32[]{:T(128)S(6)} %select_n.7, s32[]{:T(128)S(6)} %select_n.6), kind=kLoop, calls=%fused_computation | loop fusion | bytes 4423688 | tf_op jit(solution)/shard_map/dynamic_slice | solution.py:425
  28.7 3.0 %collective-permute-start.2 = (bf16[720,768]{1,0:T(8,128)(2,1)S(1)}, bf16[720,768]{1,0:T(8,128)(2,1)S(1)}, u32[]{:S(2)}, u32[]{:S(2)}) collective-permute-start(bf16[720,768]{1,0:T(8,128)(2,1)S(1)} %get-tuple-element.18), channel_id=1, source_target_pairs={{0,1},{1,0},{2,3},{3,2},{4,5},{5,4},{6,7},{7,6},{8,9},{9,8},{10,11... | collective-permute-start | bytes 3317768 | tf_op jit(solution)/shard_map/ppermute | solution.py:425
  31.7 1.9 %collective-permute-start.1 = (bf16[720,768]{1,0:T(8,128)(2,1)S(1)}, bf16[720,768]{1,0:T(8,128)(2,1)S(1)}, u32[]{:S(2)}, u32[]{:S(2)}) collective-permute-start(bf16[720,768]{1,0:T(8,128)(2,1)S(1)} %get-tuple-element.19), channel_id=1, source_target_pairs={{0,1},{1,0},{2,3},{3,2},{4,5},{5,4},{6,7},{7,6},{8,9},{9,8},{10,11... | collective-permute-start | bytes 3317768 | tf_op jit(solution)/shard_map/ppermute | solution.py:425
  33.6 2.4 %collective-permute-start = (bf16[20,32,768]{2,1,0:T(8,128)(2,1)S(1)}, bf16[20,32,768]{2,1,0:T(8,128)(2,1)S(1)}, u32[]{:S(2)}, u32[]{:S(2)}) collective-permute-start(bf16[20,32,768]{2,1,0:T(8,128)(2,1)S(1)} %bitcast.22), channel_id=1, source_target_pairs={{0,1},{1,0},{2,3},{3,2},{4,5},{5,4},{6,7},{7,6},{8,9},{9,8},{10,11... | collective-permute-start | bytes 2949128 | tf_op jit(solution)/shard_map/ppermute | solution.py:421
  36.0 2.2 %collective-permute-done.act_other_ref = bf16[20,32,768]{2,1,0:T(8,128)(2,1)S(1)} collective-permute-done((bf16[20,32,768]{2,1,0:T(8,128)(2,1)S(1)}, bf16[20,32,768]{2,1,0:T(8,128)(2,1)S(1)}, u32[]{:S(2)}, u32[]{:S(2)}) %collective-permute-start) | collective-permute-done | bytes 983072 | tf_op jit(solution)/shard_map/ppermute | solution.py:421
  38.2 0.0 collective-permute-done.2.other_high_ref
  38.2 0.0 collective-permute-done.1.other_low_ref
  38.2 3.8 %align.1 = f32[7424,128]{1,0:T(8,128)S(1)} custom-call(s32[1]{0:T(128)} %bitcast.5.core_ref, bf16[20,32,768]{2,1,0:T(8,128)(2,1)S(1)} %bitcast.23, bf16[20,32,768]{2,1,0:T(8,128)(2,1)S(1)} %collective-permute-done.act_other_ref, bf16[2880,768]{1,0:T(8,128)(2,1)S(1)} %bitcast.21, bf16[720,768]{1,0:T(8,128)(2,1)S(1)} %collective-permute-done.1.other_low_ref, ...), custom_call_target="tpu_custom_call" | custom-call | flops 2831155200 | bytes 16777216 | tf_op jit(solution)/shard_map/align/pallas_call | solution.py:428
  42.0 0.0 copy-start
  42.1 1.8 %copy-done = f32[7424,128]{1,0:T(8,128)} copy-done((f32[7424,128]{1,0:T(8,128)}, f32[7424,128]{1,0:T(8,128)S(1)}, u32[]{:S(2)}) %copy-start) | copy-done | bytes 3801112
  43.9 37.9 %all-to-all-done.refs_0_.own_ref = bf16[32,232,128]{2,1,0:T(8,128)(2,1)S(1)} async-done(((bf16[32,232,128]{2,1,0:T(8,128)(2,1)}), bf16[32,232,128]{2,1,0:T(8,128)(2,1)S(1)}, u32[]{:S(2)}, u32[]{:S(2)}) %all-to-all-start) | async-done | bytes 1900576 | tf_op jit(solution)/shard_map/all_to_all | solution.py:416
  81.8 2.9 %dots.1 = f32[64,128]{1,0:T(8,128)} custom-call(bf16[32,232,128]{2,1,0:T(8,128)(2,1)S(1)} %all-to-all-done.refs_0_.own_ref, f32[32,232,128]{2,1,0:T(8,128)} %bitcast.18), custom_call_target="tpu_custom_call" | custom-call | tf_op jit(solution)/shard_map/dots/pallas_call | solution.py:439
  84.7 3.6 %collective-permute-start.3 = (bf16[32,232,128]{2,1,0:T(8,128)(2,1)S(1)}, bf16[32,232,128]{2,1,0:T(8,128)(2,1)}, u32[]{:S(2)}, u32[]{:S(2)}) collective-permute-start(bf16[32,232,128]{2,1,0:T(8,128)(2,1)S(1)} %all-to-all-done.refs_0_.own_ref), channel_id=1, source_target_pairs={{0,1},{1,0},{2,3},{3,2},{4,5},{5,4},{6,7},{7,6},{8,9},{9,8},{10,11... | collective-permute-start | bytes 5701640 | tf_op jit(solution)/shard_map/ppermute | solution.py:454
  88.3 7.5 %all-to-all-start.1 = ((f32[64,1,128]{2,1,0:T(1,128)}), f32[64,1,128]{2,1,0:T(1,128)S(1)}, u32[]{:S(2)}, u32[]{:S(2)}) async-start(f32[64,1,128]{2,1,0:T(1,128)} %bitcast.11), calls=%async_computation.1 | async-start | bytes 65536 | tf_op jit(solution)/shard_map/all_to_all | solution.py:452
  95.8 0.0 copy-start.4
  95.8 0.0 collective-permute-done.3.other_hbm
  95.8 8.0 %project.1 = bf16[20,32,768]{2,1,0:T(8,128)(2,1)} custom-call(s32[1]{0:T(128)} %bitcast.5.core_ref, bf16[32,232,128]{2,1,0:T(8,128)(2,1)S(1)} %all-to-all-done.refs_0_.own_ref, bf16[32,232,128]{2,1,0:T(8,128)(2,1)} %collective-permute-done.3.other_hbm, bf16[2880,768]{1,0:T(8,128)(2,1)} %bitcast.20), custom_call_target="tpu_custom_call" | custom-call | flops 2831155200 | bytes 10485760 | tf_op jit(solution)/shard_map/project/pallas_call | solution.py:455
  103.8 3.7 %all-to-all-done.1 = f32[64,1,128]{2,1,0:T(1,128)S(1)} async-done(((f32[64,1,128]{2,1,0:T(1,128)}), f32[64,1,128]{2,1,0:T(1,128)S(1)}, u32[]{:S(2)}, u32[]{:S(2)}) %all-to-all-start.1) | async-done | bytes 32800 | tf_op jit(solution)/shard_map/all_to_all | solution.py:452
  107.6 0.0 copy-done.4
  107.6 0.8 collect.1
  (4 shorter events, 0.0 us)
Async XLA Ops:
  4.0 29.5 %copy-start.2 = (bf16[1,1,32,20,768]{4,2,3,1,0:T(8,128)(2,1)S(1)}, bf16[1,1,32,20,768]{4,2,3,1,0:T(8,128)(2,1)}, u32[]{:S(2)}) copy-start(bf16[1,1,32,20,768]{4,2,3,1,0:T(8,128)(2,1)} %param.9) | copy-start | bytes 2949124
  4.1 77.7 %all-to-all-start = ((bf16[32,232,128]{2,1,0:T(8,128)(2,1)}), bf16[32,232,128]{2,1,0:T(8,128)(2,1)S(1)}, u32[]{:S(2)}, u32[]{:S(2)}) async-start(bf16[32,232,128]{2,1,0:T(8,128)(2,1)} %get-tuple-element.11), calls=%async_computation | async-start | bytes 3801088 | tf_op jit(solution)/shard_map/all_to_all | solution.py:416
  26.8 11.4 %copy-start.1 = (bf16[1,768,2880]{1,2,0:T(8,128)(2,1)S(1)}, bf16[1,768,2880]{1,2,0:T(8,128)(2,1)}, u32[]{:S(2)}) copy-start(bf16[1,768,2880]{1,2,0:T(8,128)(2,1)} %param.8) | copy-start | bytes 13271044
  28.7 9.5 %collective-permute-start.2 = (bf16[720,768]{1,0:T(8,128)(2,1)S(1)}, bf16[720,768]{1,0:T(8,128)(2,1)S(1)}, u32[]{:S(2)}, u32[]{:S(2)}) collective-permute-start(bf16[720,768]{1,0:T(8,128)(2,1)S(1)} %get-tuple-element.18), channel_id=1, source_target_pairs={{0,1},{1,0},{2,3},{3,2},{4,5},{5,4},{6,7},{7,6},{8,9},{9,8},{10,11... | collective-permute-start | bytes 3317768 | tf_op jit(solution)/shard_map/ppermute | solution.py:425
  31.7 6.5 %collective-permute-start.1 = (bf16[720,768]{1,0:T(8,128)(2,1)S(1)}, bf16[720,768]{1,0:T(8,128)(2,1)S(1)}, u32[]{:S(2)}, u32[]{:S(2)}) collective-permute-start(bf16[720,768]{1,0:T(8,128)(2,1)S(1)} %get-tuple-element.19), channel_id=1, source_target_pairs={{0,1},{1,0},{2,3},{3,2},{4,5},{5,4},{6,7},{7,6},{8,9},{9,8},{10,11... | collective-permute-start | bytes 3317768 | tf_op jit(solution)/shard_map/ppermute | solution.py:425
  33.6 4.6 %collective-permute-start = (bf16[20,32,768]{2,1,0:T(8,128)(2,1)S(1)}, bf16[20,32,768]{2,1,0:T(8,128)(2,1)S(1)}, u32[]{:S(2)}, u32[]{:S(2)}) collective-permute-start(bf16[20,32,768]{2,1,0:T(8,128)(2,1)S(1)} %bitcast.22), channel_id=1, source_target_pairs={{0,1},{1,0},{2,3},{3,2},{4,5},{5,4},{6,7},{7,6},{8,9},{9,8},{10,11... | collective-permute-start | bytes 2949128 | tf_op jit(solution)/shard_map/ppermute | solution.py:421
  42.0 1.8 %copy-start = (f32[7424,128]{1,0:T(8,128)}, f32[7424,128]{1,0:T(8,128)S(1)}, u32[]{:S(2)}) copy-start(f32[7424,128]{1,0:T(8,128)S(1)} %align.1) | copy-start | bytes 11403268
  84.7 11.2 %collective-permute-start.3 = (bf16[32,232,128]{2,1,0:T(8,128)(2,1)S(1)}, bf16[32,232,128]{2,1,0:T(8,128)(2,1)}, u32[]{:S(2)}, u32[]{:S(2)}) collective-permute-start(bf16[32,232,128]{2,1,0:T(8,128)(2,1)S(1)} %all-to-all-done.refs_0_.own_ref), channel_id=1, source_target_pairs={{0,1},{1,0},{2,3},{3,2},{4,5},{5,4},{6,7},{7,6},{8,9},{9,8},{10,11... | collective-permute-start | bytes 5701640 | tf_op jit(solution)/shard_map/ppermute | solution.py:454
  88.3 19.3 %all-to-all-start.1 = ((f32[64,1,128]{2,1,0:T(1,128)}), f32[64,1,128]{2,1,0:T(1,128)S(1)}, u32[]{:S(2)}, u32[]{:S(2)}) async-start(f32[64,1,128]{2,1,0:T(1,128)} %bitcast.11), calls=%async_computation.1 | async-start | bytes 65536 | tf_op jit(solution)/shard_map/all_to_all | solution.py:452
  95.8 11.8 %copy-start.3 = (f32[32,128]{1,0:T(8,128)S(1)}, f32[32,128]{1,0:T(8,128)}, u32[]{:S(2)}) copy-start(f32[32,128]{1,0:T(8,128)} %get-tuple-element.16.refs_1_) | copy-start | bytes 49156
  95.8 11.7 %copy-start.4 = (s32[128,4]{0,1:T(4,128)S(1)}, s32[128,4]{0,1:T(4,128)}, u32[]{:S(2)}) copy-start(s32[128,4]{0,1:T(4,128)} %param.7) | copy-start | bytes 6148
